TPU v7x, 32 devices: a whole 2x2x4 slice. The times are simulated.
32 devices in a mesh: clip: 8 (over y, x, core), head: 4 (over z).
Axes of the slice: x: 2, y: 2, z: 4, core: 2. Of those that a mesh axis runs over, the one named last changes fastest.
Arguments:
- inputs: bfloat16 [6272, 768], P(('clip', 'head')), may hold values from -6 to 6
- ln1_gain: float32 [768], replicated, may hold values from 0.5 to 1.5
- ln1_bias: float32 [768], replicated, may hold values from -1.2 to 1.2
- w_qkv: bfloat16 [768, 2304], P(None, 'head'), may hold values from -0.21875 to 0.21875
- pool_kernel: float32 [8, 3, 27, 96], P('head'), may hold values from -1.75 to 1.75
- rel_table: float32 [8, 41, 96], P('head'), may hold values from -0.24 to 0.24
- comp_kernel: float32 [8, 2, 8, 96], P('head'), may hold values from -3.6 to 3.6
- memory_bank: bfloat16 [64, 2, 392, 768], P('clip', None, None, 'head'), may hold values from -6 to 6
- mem_index: int32 [16, 2], P('clip'), may hold values from 0 to 7
- clip_group: int32 [16], P('clip'), may hold values from 0 to 2
- w_proj: bfloat16 [768, 768], P('head'), may hold values from -0.21875 to 0.21875
- proj_bias: float32 [768], replicated, may hold values from -1.2 to 1.2
- ln2_gain: float32 [768], replicated, may hold values from 0.5 to 1.5
- ln2_bias: float32 [768], replicated, may hold values from -1.2 to 1.2
- w_up: bfloat16 [768, 3072], P(None, 'head'), may hold values from -0.21875 to 0.21875
- up_bias: float32 [3072], P('head'), may hold values from -1.2 to 1.2
- w_down: bfloat16 [3072, 768], P('head'), may hold values from -0.109375 to 0.109375
- down_bias: float32 [768], replicated, may hold values from -1.2 to 1.2
- cotangent: bfloat16 [6272, 768], P(('clip', 'head')), may hold values from -6 to 6
Outputs:
- output: bfloat16 [6272, 768], P(('clip', 'head'))
- grad_inputs: float32 [6272, 768], P(('clip', 'head'))
- grad_ln1_gain: float32 [768], replicated
- grad_ln1_bias: float32 [768], replicated
- grad_w_qkv: float32 [768, 2304], P(None, 'head')
- grad_pool_kernel: float32 [8, 3, 27, 96], P('head')
- grad_rel_table: float32 [8, 41, 96], P('head')
- grad_comp_kernel: float32 [8, 2, 8, 96], P('head')
- grad_w_proj: float32 [768, 768], P('head')
- grad_proj_bias: float32 [768], replicated
- grad_ln2_gain: float32 [768], replicated
- grad_ln2_bias: float32 [768], replicated
- grad_w_up: float32 [768, 3072], P(None, 'head')
- grad_up_bias: float32 [3072], P('head')
- grad_w_down: float32 [3072, 768], P('head')
- grad_down_bias: float32 [768], replicated
Inputs may be any that keep to these rules, and one draw needn't show every extreme that they name: mem_index names rows of the memory bank held by the clip's own index of the clip axis. clip_group 0, 1, 2 selects memory stride 2, 4, 8.
All inputs are finite; a program needn't handle non-finite values.
Results may differ from a plain program's by a relative error of at most 0.02.
The roundings to bfloat16 on the way count: a program that leaves them out, or rounds other values in their place, can miss the bound.
Values may be sent and summed in bfloat16 or wider, within the bound.
No kernel may reach another device: no remote copies, remote signals or barrier semaphores. Data moves between devices by JAX's collectives and lax.ppermute only.
A program may use at most 256 MiB of HBM per device.

v0:
```python
import jax
import jax.numpy as jnp
from jax import lax
from jax.sharding import PartitionSpec as P

highest = lax.Precision.HIGHEST
eps_norm = 1e-06
neg_large = -1000000000.0


def layer_norm(values_in, gain_vec, shift_vec):
    row_mean = jnp.mean(values_in, axis=-1, keepdims=True)
    centered = values_in - row_mean
    row_var = jnp.mean(centered * centered, axis=-1, keepdims=True)
    return centered * lax.rsqrt(row_var + eps_norm) * gain_vec + shift_vec


def offsets(length_of, span_of, middle):
    places = jnp.arange(length_of)
    slots = jnp.arange(span_of)
    return (places[:, None, None] - places[None, :, None] + middle == slots[None, None, :]).astype(
        jnp.float32
    )


def pool_grid(field, kernel):
    padded = jnp.pad(field, ((0, 0), (1, 1), (1, 1), (1, 1), (0, 0), (0, 0), (0, 0)))
    total = jnp.zeros_like(field)
    for tap_index in range(27):
        shift_t = tap_index // 9
        shift_h = tap_index // 3 % 3
        shift_w = tap_index % 3
        total = (
            total
            + padded[:, shift_t : shift_t + 8, shift_h : shift_h + 7, shift_w : shift_w + 7]
            * kernel[:, :, tap_index, :]
        )
    return total


def rel_bias(queries, table):
    clip_count = queries.shape[0]
    head_count = queries.shape[2]
    projected = jnp.einsum("nqhd,hrd->nhqr", queries, table, precision=highest).reshape(
        clip_count, head_count, 8, 7, 7, 41
    )
    along_t = jnp.einsum(
        "nhaber,akr->nhabek", projected[..., 0:15], offsets(8, 15, 7), precision=highest
    )
    along_h = jnp.einsum(
        "nhaber,bkr->nhabek", projected[..., 15:28], offsets(7, 13, 6), precision=highest
    )
    along_w = jnp.einsum(
        "nhaber,ekr->nhabek", projected[..., 28:41], offsets(7, 13, 6), precision=highest
    )
    total = along_t[..., :, None, None] + along_h[..., None, :, None] + along_w[..., None, None, :]
    return total.reshape(clip_count, head_count, 392, 392)


def stride_tables():
    out_frame = jnp.arange(4)[:, None, None]
    frames = jnp.arange(8)[None, :, None]
    tap_index = jnp.arange(8)[None, None, :]
    tables = []
    for section_level in range(3):
        stride = 2 ** (section_level + 1)
        allowed = (
            (frames == stride * out_frame + tap_index)
            & (tap_index < stride)
            & (out_frame < 8 // stride)
        )
        tables.append(allowed.astype(jnp.float32))
    return jnp.stack(tables)


def group_select(group_ids):
    return (group_ids[:, None] == jnp.arange(3)[None, :]).astype(jnp.float32)


def compress(bank, kernel, index_rows, group_ids):
    head_count = kernel.shape[0]
    head_size = kernel.shape[3]
    clip_count = index_rows.shape[0]
    chosen = (
        jnp.take(bank, index_rows, axis=0)
        .astype(jnp.float32)
        .reshape(clip_count, 2, 2, 8, 49, head_count, head_size)
    )
    pattern = jnp.einsum(
        "ng,gtfj->ntfj", group_select(group_ids), stride_tables(), precision=highest
    )
    coeffs = jnp.einsum("ntfj,hkjd->nktfhd", pattern, kernel, precision=highest)
    packed = jnp.einsum("nktfhd,nmkfshd->knmtshd", coeffs, chosen, precision=highest)
    packed = packed.reshape(2, clip_count, 392, head_count, head_size)
    return (packed[0], packed[1])


def memory_valid(group_ids):
    clip_count = group_ids.shape[0]
    limits = jnp.sum(
        group_select(group_ids) * jnp.array([4.0, 2.0, 1.0], dtype=jnp.float32), axis=-1
    )
    slot_pos = jnp.arange(4).astype(jnp.float32)
    allowed = slot_pos[None, :] < limits[:, None]
    return jnp.broadcast_to(allowed[:, None, :, None], (clip_count, 2, 4, 49)).reshape(
        clip_count, 392
    )


def gelu_exact(values_in):
    return jax.nn.gelu(values_in, approximate=False)


def on_device(
    inputs,
    ln1_gain,
    ln1_bias,
    w_qkv,
    pool_kernel,
    rel_table,
    comp_kernel,
    memory_bank,
    mem_index,
    clip_group,
    w_proj,
    proj_bias,
    ln2_gain,
    ln2_bias,
    w_up,
    up_bias,
    w_down,
    down_bias,
    cotangent,
):
    clip_count = clip_group.shape[0]
    head_count = pool_kernel.shape[0]
    head_size = pool_kernel.shape[3]
    score_scale = head_size ** (-0.5)
    f_type = jnp.float32
    b_type = jnp.bfloat16
    token_rows = inputs.astype(f_type)
    norm1, norm1_back = jax.vjp(layer_norm, token_rows, ln1_gain, ln1_bias)
    norm1_low = norm1.astype(b_type)
    gathered1 = lax.all_gather(norm1_low, "head", axis=0, tiled=True)
    qkv = jnp.dot(gathered1, w_qkv, preferred_element_type=f_type).reshape(
        clip_count, 8, 7, 7, head_count, 3, head_size
    )
    pooled, pool_back = jax.vjp(pool_grid, qkv, pool_kernel)
    pooled = pooled.reshape(clip_count, 392, head_count, 3, head_size).astype(b_type)
    queries = pooled[..., 0, :]
    key_part = pooled[..., 1, :]
    value_part = pooled[..., 2, :]
    (mem_keys, mem_values), comp_back = jax.vjp(
        lambda kern: compress(memory_bank, kern, mem_index, clip_group), comp_kernel
    )
    all_keys = jnp.concatenate([key_part, mem_keys.astype(b_type)], axis=1)
    all_values = jnp.concatenate([value_part, mem_values.astype(b_type)], axis=1)
    queries_wide = queries.astype(f_type)
    rel_terms, rel_back = jax.vjp(rel_bias, queries_wide, rel_table)
    key_mask = jnp.concatenate(
        [jnp.ones((clip_count, 392), dtype=bool), memory_valid(clip_group)], axis=1
    )
    scores = (
        jnp.einsum("nqhd,nkhd->nhqk", queries, all_keys, preferred_element_type=f_type)
        * score_scale
    )
    scores = jnp.concatenate([scores[..., :392] + rel_terms, scores[..., 392:]], axis=-1)
    scores = jnp.where(key_mask[:, None, None, :], scores, neg_large)
    attn_probs = jax.nn.softmax(scores, axis=-1)
    probs_low = attn_probs.astype(b_type)
    attended = jnp.einsum("nhqk,nkhd->nqhd", probs_low, all_values, preferred_element_type=f_type)
    head_out = (
        (attended + queries_wide).astype(b_type).reshape(clip_count * 392, head_count * head_size)
    )
    branch = (
        lax.psum_scatter(
            jnp.dot(head_out, w_proj, preferred_element_type=f_type).astype(jnp.bfloat16),
            "head",
            scatter_dimension=0,
            tiled=True,
        ).astype(jnp.float32)
        + proj_bias
    )
    midway = token_rows + branch
    norm2, norm2_back = jax.vjp(layer_norm, midway, ln2_gain, ln2_bias)
    norm2_low = norm2.astype(b_type)
    gathered2 = lax.all_gather(norm2_low, "head", axis=0, tiled=True)
    hidden = jnp.dot(gathered2, w_up, preferred_element_type=f_type) + up_bias
    activated, gelu_back = jax.vjp(gelu_exact, hidden)
    act_low = activated.astype(b_type)
    mlp_out = lax.psum_scatter(
        jnp.dot(act_low, w_down, preferred_element_type=f_type).astype(jnp.bfloat16),
        "head",
        scatter_dimension=0,
        tiled=True,
    ).astype(jnp.float32)
    output = (midway + mlp_out + down_bias).astype(b_type)
    rows_attn, rows_mlp = (
        lax.all_gather(norm1_low, "head", axis=0, tiled=True),
        lax.all_gather(norm2_low, "head", axis=0, tiled=True),
    )
    grad_top = lax.all_gather(cotangent, "head", axis=0, tiled=True)
    grad_act = jnp.dot(grad_top, w_down.T, preferred_element_type=f_type)
    g_w_down = jnp.dot(act_low.T, grad_top, preferred_element_type=f_type)
    (grad_hidden,) = gelu_back(grad_act)
    grad_hidden_low = grad_hidden.astype(b_type)
    g_up_bias = jnp.sum(grad_hidden_low.astype(f_type), axis=0)
    g_w_up = jnp.dot(rows_mlp.T, grad_hidden_low, preferred_element_type=f_type)
    grad_norm2 = lax.psum_scatter(
        jnp.dot(grad_hidden_low, w_up.T, preferred_element_type=f_type).astype(jnp.bfloat16),
        "head",
        scatter_dimension=0,
        tiled=True,
    ).astype(jnp.float32)
    grad_mid_norm, g_ln2_gain, g_ln2_bias = norm2_back(grad_norm2)
    grad_local = cotangent.astype(f_type)
    grad_mid = grad_local + grad_mid_norm
    g_down_bias = jnp.sum(grad_local, axis=0)
    grad_branch_low = grad_mid.astype(b_type)
    g_proj_bias = jnp.sum(grad_branch_low.astype(f_type), axis=0)
    grad_branch = lax.all_gather(grad_branch_low, "head", axis=0, tiled=True)
    grad_heads = jnp.dot(grad_branch, w_proj.T, preferred_element_type=f_type).reshape(
        clip_count, 392, head_count, head_size
    )
    g_w_proj = jnp.dot(head_out.T, grad_branch, preferred_element_type=f_type)
    grad_att_low = grad_heads.astype(b_type)
    grad_probs = jnp.einsum(
        "nqhd,nkhd->nhqk", grad_att_low, all_values, preferred_element_type=f_type
    )
    grad_values = jnp.einsum(
        "nhqk,nqhd->nkhd", probs_low, grad_att_low, preferred_element_type=f_type
    )
    grad_scores = attn_probs * (
        grad_probs - jnp.sum(attn_probs * grad_probs, axis=-1, keepdims=True)
    )
    grad_scores_low = grad_scores.astype(b_type)
    grad_queries = (
        jnp.einsum("nhqk,nkhd->nqhd", grad_scores_low, all_keys, preferred_element_type=f_type)
        * score_scale
        + grad_heads
    )
    grad_keys = (
        jnp.einsum("nhqk,nqhd->nkhd", grad_scores_low, queries, preferred_element_type=f_type)
        * score_scale
    )
    grad_query_rel, g_rel = rel_back(grad_scores_low[..., :392].astype(f_type))
    grad_queries = grad_queries + grad_query_rel
    (g_comp,) = comp_back((grad_keys[:, 392:], grad_values[:, 392:]))
    grad_pooled = jnp.stack([grad_queries, grad_keys[:, :392], grad_values[:, :392]], axis=3)
    grad_qkv, g_pool = pool_back(grad_pooled.reshape(clip_count, 8, 7, 7, head_count, 3, head_size))
    grad_qkv_low = grad_qkv.reshape(clip_count * 392, head_count * 3 * head_size).astype(b_type)
    g_w_qkv = jnp.dot(rows_attn.T, grad_qkv_low, preferred_element_type=f_type)
    grad_norm1 = lax.psum_scatter(
        jnp.dot(grad_qkv_low, w_qkv.T, preferred_element_type=f_type).astype(jnp.bfloat16),
        "head",
        scatter_dimension=0,
        tiled=True,
    ).astype(jnp.float32)
    grad_in_norm, g_ln1_gain, g_ln1_bias = norm1_back(grad_norm1)
    grad_inputs = grad_mid + grad_in_norm
    g_w_qkv, g_pool, g_rel, g_comp, g_w_proj, g_w_up, g_up_bias, g_w_down = (
        lax.psum(g_w_qkv.astype(jnp.bfloat16), "clip").astype(jnp.float32),
        lax.psum(g_pool.astype(jnp.bfloat16), "clip").astype(jnp.float32),
        lax.psum(g_rel.astype(jnp.bfloat16), "clip").astype(jnp.float32),
        lax.psum(g_comp.astype(jnp.bfloat16), "clip").astype(jnp.float32),
        lax.psum(g_w_proj.astype(jnp.bfloat16), "clip").astype(jnp.float32),
        lax.psum(g_w_up.astype(jnp.bfloat16), "clip").astype(jnp.float32),
        lax.psum(g_up_bias.astype(jnp.bfloat16), "clip").astype(jnp.float32),
        lax.psum(g_w_down.astype(jnp.bfloat16), "clip").astype(jnp.float32),
    )
    g_ln1_gain, g_ln1_bias, g_proj_bias, g_ln2_gain, g_ln2_bias, g_down_bias = lax.psum(
        (g_ln1_gain, g_ln1_bias, g_proj_bias, g_ln2_gain, g_ln2_bias, g_down_bias), ("clip", "head")
    )
    return (
        output,
        grad_inputs,
        g_ln1_gain,
        g_ln1_bias,
        g_w_qkv,
        g_pool,
        g_rel,
        g_comp,
        g_w_proj,
        g_proj_bias,
        g_ln2_gain,
        g_ln2_bias,
        g_w_up,
        g_up_bias,
        g_w_down,
        g_down_bias,
    )


def solution(mesh):
    return jax.shard_map(
        on_device,
        mesh=mesh,
        in_specs=(
            P(("clip", "head"), None),
            P(),
            P(),
            P(None, "head"),
            P("head", None, None, None),
            P("head", None, None),
            P("head", None, None, None),
            P("clip", None, None, "head"),
            P("clip", None),
            P("clip"),
            P("head", None),
            P(),
            P(),
            P(),
            P(None, "head"),
            P("head"),
            P("head", None),
            P(),
            P(("clip", "head"), None),
        ),
        out_specs=(
            P(("clip", "head"), None),
            P(("clip", "head"), None),
            P(),
            P(),
            P(None, "head"),
            P("head", None, None, None),
            P("head", None, None),
            P("head", None, None, None),
            P("head", None),
            P(),
            P(),
            P(),
            P(None, "head"),
            P("head"),
            P("head", None),
            P(),
        ),
        check_vma=False,
    )
```

profile of v0, /device:TPU:0, one launch (start us, length us, event | category | flops | bytes accessed | tf_op | source)
XLA Modules:
  0.0 790.5 jit_solution(8424858933768300924)
XLA Ops:
  24.2 3.9 copy.181
  28.2 4.0 gather.7
  34.8 5.4 copy.183
  40.2 5.6 fusion.17
  59.2 3.6 reshape.540
  63.1 32.8 %add_convert_fusion = bf16[2,8,7,7,2,3,96]{6,5,4,3,2,1,0:T(4,128)(2,1)S(1)} fusion(f32[2,8,7,7,2,3,96]{6,5,4,3,2,1,0:T(4,128)} %reshape.540, f32[2,3,96]{2,1,0:T(4,128)S(1)} %copy.178, f32[2,3,96]{2,1,0:T(4,128)S(1)} %copy.177, f32[2,3,96]{2,1,0:T(4,128)S(1)} %copy.176, f32[2,3,96]{2,1,0:T(4,128)S(1)} %copy.175, f32[2,3,96]{2,1,0:T(4,128)S(1)} %copy.174, ...), kind=kLoop, calls=%fused_computation.71 | loop fusion | flops 24385536 | bytes 2771712 | tf_op jit(solution)/shard_map/convert_element_type | solution.py:149
  101.9 2.9 fusion.121
  104.8 6.2 convolution_bitcast_fusion.2
  112.4 6.6 convolution_bitcast_fusion.6
  121.1 5.4 convolution_bitcast_fusion.5
  127.7 2.8 broadcast_add_fusion.1
  130.6 17.2 %broadcast_add_fusion = f32[2,2,8,7,7,8,7,7]{7,6,5,4,3,2,1,0:T(8,128)} fusion(f32[2,2,8,7,7,7]{5,4,3,2,1,0:T(8,128)S(1)} %copy.199, f32[2,2,8,7,7,8,7]{6,5,4,3,2,1,0:T(8,128)S(1)} %broadcast_add_fusion.1), kind=kLoop, calls=%fused_computation.28 | loop fusion | flops 614656 | bytes 2853760 | tf_op jit(solution)/shard_map/jvp()/add | solution.py:56
  147.8 35.3 %add.487 = f32[2,2,392,392]{3,2,1,0:T(8,128)} reshape(f32[2,2,8,7,7,8,7,7]{7,6,5,4,3,2,1,0:T(8,128)} %broadcast_add_fusion) | data formatting | bytes 4917248 | tf_op jit(solution)/shard_map/jvp()/add | solution.py:56
  186.4 10.5 %fusion.122 = (f32[2,2,392]{2,1,0:T(2,128)S(1)}, f32[2,2,392,784]{3,2,1,0:T(8,128)}) fusion(f32[2,2,392,392]{3,2,1,0:T(8,128)S(1)} %get-tuple-element.139, f32[2,2,392,392]{3,2,1,0:T(8,128)S(1)} %get-tuple-element.138, pred[2,784]{1,0:T(4,128)(4,1)S(1)} %concatenate.14), kind=kOutput, calls=%fused_computation.320 | output fusion | flops 4918031 | bytes 9842336 | tf_op jit(solution)/shard_map/sub | solution.py:169
  196.9 17.4 %fusion.31 = bf16[2,392,2,96]{1,3,2,0:T(8,128)(2,1)S(1)} fusion(bf16[2,392,2,96]{1,3,2,0:T(8,128)(2,1)S(1)} %copy-done.43, bf16[2,392,2,96]{1,3,2,0:T(8,128)(2,1)S(1)} %bitcast.321, bf16[2,392,2,1,96]{1,4,2,0,3:T(8,128)(2,1)S(1)} %copy.246, f32[2,2,392]{2,1,0:T(2,128)S(1)} %get-tuple-element.208, f32[2,2,392,392]{3,2,1,0:T(8,128)} %copy-done.6, ...), kind=kOutput, calls=%fused_computation.153 | convolution fusion | flops 243832624 | bytes 6129312 | tf_op jit(solution)/shard_map/nhqk,nkhd->nqhd/dot_general | solution.py:171
  215.7 30.0 %fusion = bf16[200,768]{1,0:T(8,128)(2,1)S(1)} fusion(bf16[784,768]{1,0:T(8,128)(2,1)S(1)} %convolution_convert_fusion.3), kind=kCustom, calls=%all-reduce-scatter | all-reduce-scatter fusion | flops 614401 | bytes 1511936
  252.3 30.0 %all-gather.11.cloned.1.call-done = bf16[4,196,768]{2,1,0:T(8,128)(2,1)} async-done(((bf16[1,196,768]{2,1,0:T(8,128)(2,1)}), bf16[4,196,768]{2,1,0:T(8,128)(2,1)}) %all-gather.11.cloned.1.call-update) | async-done | bytes 1204240 | tf_op jit(solution)/shard_map/all_gather | solution.py:187
  283.8 2.8 fusion.124
  286.7 8.1 %fusion.115 = (bf16[768]{0:T(1024)(128)(2,1)}, bf16[784,768]{1,0:T(8,128)(2,1)S(1)}, f32[784,768]{1,0:T(8,128)}) fusion(f32[784,768]{1,0:T(8,128)S(1)} %fusion.124, f32[768]{0:T(1024)S(1)} %copy-done.118, bf16[784,768]{1,0:T(8,128)(2,1)S(1)} %reshape.567, bf16[768,768]{1,0:T(8,128)(2,1)S(1)} %copy-done.122), kind=kOutput, calls=%fused_computation.315 | convolution fusion | flops 969399552 | bytes 8409600 | tf_op jit(solution)/shard_map/dot_general | solution.py:203
  296.9 27.2 %fusion.1 = bf16[200,768]{1,0:T(8,128)(2,1)S(1)} fusion(bf16[784,768]{1,0:T(8,128)(2,1)S(1)} %convolution_convert_fusion.1), kind=kCustom, calls=%all-reduce-scatter.1 | all-reduce-scatter fusion | flops 614401 | bytes 1511936
  331.2 2.7 multiply_convert_fusion.1
  334.0 3.6 convolution_convert_fusion.2
  342.5 20.0 %all-gather.15.cloned.1.call-done = bf16[4,196,768]{2,1,0:T(8,128)(2,1)} async-done(((bf16[1,196,768]{2,1,0:T(8,128)(2,1)}), bf16[4,196,768]{2,1,0:T(8,128)(2,1)}) %all-gather.15.cloned.1.call-update) | async-done | bytes 1204240 | tf_op jit(solution)/shard_map/all_gather | solution.py:221
  366.9 19.1 %convolution_bitcast_fusion.1 = f32[2,784,2,96]{1,3,2,0:T(8,128)} fusion(f32[2,392,2,96]{1,0,3,2:T(2,128)S(1)} %reshape.544, f32[2,2,392]{2,1,0:T(2,128)S(1)} %get-tuple-element.208, f32[2,2,392,392]{3,2,1,0:T(8,128)} %copy-done.6, f32[2,2,392,392]{3,2,1,0:T(8,128)} %copy-done.5, pred[2,784]{1,0:T(4,128)(4,1)S(1)} %concatenate.14), kind=kOutput, calls=%fused_computation.134 | convolution fusion | flops 242176816 | bytes 6731424 | tf_op jit(solution)/shard_map/nhqk,nqhd->nkhd/dot_general | solution.py:230
  386.0 4.0 multiply_reduce_fusion
  403.2 49.6 %reshape.550 = f32[2,2,8,7,7,8,7,7]{7,6,5,4,3,2,1,0:T(8,128)} reshape(f32[2,2,392,392]{3,2,1,0:T(8,128)} %slice_convert_fusion) | data formatting | bytes 4917248 | tf_op jit(solution)/shard_map/transpose(jvp())/reshape | solution.py:57
  452.8 31.2 %fusion.113 = (f32[2,2,8,7,7,7]{5,4,3,2,1,0:T(8,128)}, f32[2,2,8,7,7,8]{5,4,3,2,1,0:T(8,128)S(1)}, f32[2,2,8,7,7,7]{5,4,3,2,1,0:T(8,128)S(1)}) fusion(f32[2,2,8,7,7,8,7,7]{7,6,5,4,3,2,1,0:T(8,128)} %reshape.550), kind=kLoop, calls=%fused_computation.314 | loop fusion | flops 1809472 | bytes 2596608 | tf_op jit(solution)/shard_map/transpose(jvp())/reduce_sum | solution.py:56
  493.1 18.9 %multiply_reduce_fusion.21 = (f32[2,3,96]{2,1,0:T(4,128)}, f32[2,3,96]{2,1,0:T(4,128)}, f32[2,3,96]{2,1,0:T(4,128)}, f32[2,3,96]{2,1,0:T(4,128)}, f32[2,3,96]{2,...) fusion(f32[2,8,7,7,2,3,96]{6,5,4,3,2,1,0:T(4,128)} %reshape.540, ...), kind=kLoop, calls=%fused_computation.64 | loop fusion | flops 9929088 | bytes 3635712 | tf_op jit(solution)/shard_map/transpose(jvp())/reduce_sum | solution.py:35
  512.0 3.9 broadcast_multiply_fusion.19
  515.9 12.5 %multiply_reduce_fusion.25 = (f32[2,3,96]{2,1,0:T(4,128)S(1)}, f32[2,3,96]{2,1,0:T(4,128)S(1)}, f32[2,3,96]{2,1,0:T(4,128)S(1)}, f32[2,3,96]{2,1,0:T(4,128)S(1)}...) fusion(f32[2,8,7,7,2,3,96]{6,5,4,3,2,1,0:T(4,128)S(1)} %copy-do, ...), kind=kLoop, calls=%fused_computation.68 | loop fusion | flops 8575488 | bytes 5439744 | tf_op jit(solution)/shard_map/transpose(jvp())/reduce_sum | solution.py:35
  528.4 12.6 %multiply_reduce_fusion.23 = (f32[2,3,96]{2,1,0:T(4,128)S(1)}, f32[2,3,96]{2,1,0:T(4,128)S(1)}, f32[2,3,96]{2,1,0:T(4,128)S(1)}, f32[2,3,96]{2,1,0:T(4,128)}, f3...) fusion(f32[2,8,7,7,2,3,96]{6,5,4,3,2,1,0:T(4,128)S(1)} %copy-do, ...), kind=kLoop, calls=%fused_computation.66 | loop fusion | flops 8575488 | bytes 5439744 | tf_op jit(solution)/shard_map/transpose(jvp())/reduce_sum | solution.py:35
  541.1 6.6 broadcast_multiply_fusion.5
  547.8 6.5 broadcast_multiply_fusion.4
  554.4 6.5 broadcast_multiply_fusion.3
  560.9 6.5 broadcast_multiply_fusion.2
  567.5 6.7 broadcast_multiply_fusion.1
  574.2 7.1 pad_maximum_fusion
  581.3 26.9 %pad_add_fusion = f32[2,10,9,9,2,3,96]{6,5,4,3,2,1,0:T(4,128)} fusion(f32[2,8,7,7,2,3,96]{6,5,4,3,2,1,0:T(4,128)} %get-tuple-element.143, f32[2,8,7,7,2,3,96]{6,5,4,3,2,1,0:T(4,128)} %get-tuple-element.142, f32[2,8,7,7,2,3,96]{6,5,4,3,2,1,0:T(4,128)} %get-tuple-element.141, f32[2,8,7,7,2,3,96]{6,5,4,3,2,1,0:T(4,128)} %broadcast_multiply_fusion.19, ...), kind=kLoop, calls=%fused_computation.29 | loop fusion | flops 19595520 | bytes 43471872 | tf_op jit(solution)/shard_map/transpose(jvp())/add_any | solution.py:35
  608.1 6.5 fusion.6
  616.6 3.3 convolution_convert_fusion.7
  619.9 3.7 convolution_convert_fusion.4
  627.7 4.4 copy.219
  632.1 7.4 convolution_bitcast_fusion
  639.5 4.8 stack.29
  644.3 46.6 %fusion.114 = (bf16[200,768]{1,0:T(8,128)(2,1)}, bf16[200,768]{1,0:T(8,128)(2,1)}) fusion(bf16[784,768]{1,0:T(8,128)(2,1)} %convolution_convert_fusion.2, bf16[784,768]{1,0:T(8,128)(2,1)} %convolution_convert_fusion.4), kind=kCustom, calls=%all-reduce-scatter.4 | all-reduce-scatter fusion | flops 1228801 | bytes 3023360
  701.2 3.1 fusion.41
  705.1 24.3 %all-reduce.70 = (bf16[2,3,27,96]{3,1,0,2:T(4,128)(2,1)S(1)}, bf16[2,41,96]{2,1,0:T(8,128)(2,1)S(1)}, bf16[2,2,8,96]{3,2,1,0:T(8,128)(2,1)S(1)}, bf16[768]{0:T(1024)(128)(2,1)S(1)}) all-reduce(bf16[2,3,27,96]{3,1,0,2:T(4,128)(2,1)S(1)} %add_convert_fusion.4, ...), channel_id=1, replica_groups=mesh['clip'=8,'head'=4] {'clip'}, use_global_device_ids=true, to_apply=%region_51.52 | all-reduce | flops 27264 | bytes 109056 | tf_op jit(solution)/shard_map/psum | solution.py:263
  736.7 39.2 %all-reduce.69 = (f32[768]{0:T(1024)}, f32[768]{0:T(1024)}, f32[768]{0:T(1024)}, f32[768]{0:T(1024)}, f32[768]{0:T(1024)}, /*index=5*/f32[768]{0:T(1024)}) all-reduce(f32[768]{0:T(1024)S(1)} %get-tuple-element.95, f32[768]{0:T(1024)S(1)} %get-tuple-element.98, ...), channel_id=1, replica_groups=mesh['clip'=8,'head'=4] {'clip','head'}, use_global_device_ids=true, to_apply=%region_20.21 | all-reduce | flops 4608 | bytes 36864 | tf_op jit(solution)/shard_map/psum | solution.py:271
  (429 shorter events, 127.6 us)
Async XLA Ops:
  7.2 47.0 %all-gather.9.cloned.1.call-start = ((), (), s32[]{:S(2)}) async-start(), calls=%async_computation | async-start | bytes 1536000 | tf_op jit(solution)/shard_map/all_gather | solution.py:144
  12.8 238.1 %all-gather.13.cloned.1.call-start = ((), (), s32[]{:S(2)}) async-start(), calls=%async_computation.2 | async-start | bytes 1536000 | tf_op jit(solution)/shard_map/all_gather | solution.py:202
  13.6 268.8 %all-gather.11.cloned.1.call-start = ((), (), s32[]{:S(2)}) async-start(), calls=%async_computation.1 | async-start | bytes 1536000 | tf_op jit(solution)/shard_map/all_gather | solution.py:187
  18.2 44.6 %copy-start.70 = (f32[2,3,96]{2,1,0:T(4,128)}, f32[2,3,96]{2,1,0:T(4,128)S(1)}, u32[]{:S(2)}) copy-start(f32[2,3,96]{2,1,0:T(4,128)S(1)} %copy.153) | copy-start | bytes 6916
  18.2 44.6 %copy-start.56 = (f32[2,3,96]{2,1,0:T(4,128)}, f32[2,3,96]{2,1,0:T(4,128)S(1)}, u32[]{:S(2)}) copy-start(f32[2,3,96]{2,1,0:T(4,128)S(1)} %copy.158) | copy-start | bytes 6916
  18.3 44.6 %copy-start.58 = (f32[2,3,96]{2,1,0:T(4,128)}, f32[2,3,96]{2,1,0:T(4,128)S(1)}, u32[]{:S(2)}) copy-start(f32[2,3,96]{2,1,0:T(4,128)S(1)} %copy.157) | copy-start | bytes 6916
  18.3 44.5 %copy-start.60 = (f32[2,3,96]{2,1,0:T(4,128)}, f32[2,3,96]{2,1,0:T(4,128)S(1)}, u32[]{:S(2)}) copy-start(f32[2,3,96]{2,1,0:T(4,128)S(1)} %copy.156) | copy-start | bytes 6916
  18.3 44.5 %copy-start.62 = (f32[2,3,96]{2,1,0:T(4,128)}, f32[2,3,96]{2,1,0:T(4,128)S(1)}, u32[]{:S(2)}) copy-start(f32[2,3,96]{2,1,0:T(4,128)S(1)} %copy.155) | copy-start | bytes 6916
  18.3 44.5 %copy-start.66 = (f32[2,3,96]{2,1,0:T(4,128)}, f32[2,3,96]{2,1,0:T(4,128)S(1)}, u32[]{:S(2)}) copy-start(f32[2,3,96]{2,1,0:T(4,128)S(1)} %copy.154) | copy-start | bytes 6916
  18.3 44.5 %copy-start.72 = (f32[2,3,96]{2,1,0:T(4,128)}, f32[2,3,96]{2,1,0:T(4,128)S(1)}, u32[]{:S(2)}) copy-start(f32[2,3,96]{2,1,0:T(4,128)S(1)} %copy.178) | copy-start | bytes 6916
  18.4 44.5 %copy-start.74 = (f32[2,3,96]{2,1,0:T(4,128)}, f32[2,3,96]{2,1,0:T(4,128)S(1)}, u32[]{:S(2)}) copy-start(f32[2,3,96]{2,1,0:T(4,128)S(1)} %copy.177) | copy-start | bytes 6916
  19.5 43.3 %copy-start.76 = (f32[2,3,96]{2,1,0:T(4,128)}, f32[2,3,96]{2,1,0:T(4,128)S(1)}, u32[]{:S(2)}) copy-start(f32[2,3,96]{2,1,0:T(4,128)S(1)} %copy.152) | copy-start | bytes 6916
  19.6 43.3 %copy-start.78 = (f32[2,3,96]{2,1,0:T(4,128)}, f32[2,3,96]{2,1,0:T(4,128)S(1)}, u32[]{:S(2)}) copy-start(f32[2,3,96]{2,1,0:T(4,128)S(1)} %copy.176) | copy-start | bytes 6916
  19.6 43.3 %copy-start.82 = (f32[2,3,96]{2,1,0:T(4,128)}, f32[2,3,96]{2,1,0:T(4,128)S(1)}, u32[]{:S(2)}) copy-start(f32[2,3,96]{2,1,0:T(4,128)S(1)} %copy.175) | copy-start | bytes 6916
  19.6 43.3 %copy-start.100 = (f32[2,3,96]{2,1,0:T(4,128)}, f32[2,3,96]{2,1,0:T(4,128)S(1)}, u32[]{:S(2)}) copy-start(f32[2,3,96]{2,1,0:T(4,128)S(1)} %copy.174) | copy-start | bytes 6916
  19.6 43.3 %copy-start.104 = (f32[2,3,96]{2,1,0:T(4,128)}, f32[2,3,96]{2,1,0:T(4,128)S(1)}, u32[]{:S(2)}) copy-start(f32[2,3,96]{2,1,0:T(4,128)S(1)} %copy.173) | copy-start | bytes 6916
  19.6 43.3 %copy-start.106 = (f32[2,3,96]{2,1,0:T(4,128)}, f32[2,3,96]{2,1,0:T(4,128)S(1)}, u32[]{:S(2)}) copy-start(f32[2,3,96]{2,1,0:T(4,128)S(1)} %copy.172) | copy-start | bytes 6916
  19.7 43.3 %copy-start.108 = (f32[2,3,96]{2,1,0:T(4,128)}, f32[2,3,96]{2,1,0:T(4,128)S(1)}, u32[]{:S(2)}) copy-start(f32[2,3,96]{2,1,0:T(4,128)S(1)} %copy.171) | copy-start | bytes 6916
  19.7 43.3 %copy-start.96 = (f32[2,3,96]{2,1,0:T(4,128)}, f32[2,3,96]{2,1,0:T(4,128)S(1)}, u32[]{:S(2)}) copy-start(f32[2,3,96]{2,1,0:T(4,128)S(1)} %copy.170) | copy-start | bytes 6916
  19.7 43.3 %copy-start.98 = (f32[2,3,96]{2,1,0:T(4,128)}, f32[2,3,96]{2,1,0:T(4,128)S(1)}, u32[]{:S(2)}) copy-start(f32[2,3,96]{2,1,0:T(4,128)S(1)} %copy.169) | copy-start | bytes 6916
  19.7 43.2 %copy-start.102 = (f32[2,3,96]{2,1,0:T(4,128)}, f32[2,3,96]{2,1,0:T(4,128)S(1)}, u32[]{:S(2)}) copy-start(f32[2,3,96]{2,1,0:T(4,128)S(1)} %copy.168) | copy-start | bytes 6916
  19.7 43.2 %copy-start.90 = (f32[2,3,96]{2,1,0:T(4,128)}, f32[2,3,96]{2,1,0:T(4,128)S(1)}, u32[]{:S(2)}) copy-start(f32[2,3,96]{2,1,0:T(4,128)S(1)} %copy.167) | copy-start | bytes 6916
  19.8 43.2 %copy-start.92 = (f32[2,3,96]{2,1,0:T(4,128)}, f32[2,3,96]{2,1,0:T(4,128)S(1)}, u32[]{:S(2)}) copy-start(f32[2,3,96]{2,1,0:T(4,128)S(1)} %copy.166) | copy-start | bytes 6916
  19.8 43.2 %copy-start.94 = (f32[2,3,96]{2,1,0:T(4,128)}, f32[2,3,96]{2,1,0:T(4,128)S(1)}, u32[]{:S(2)}) copy-start(f32[2,3,96]{2,1,0:T(4,128)S(1)} %copy.165) | copy-start | bytes 6916
  19.8 43.2 %copy-start.84 = (f32[2,3,96]{2,1,0:T(4,128)}, f32[2,3,96]{2,1,0:T(4,128)S(1)}, u32[]{:S(2)}) copy-start(f32[2,3,96]{2,1,0:T(4,128)S(1)} %copy.164) | copy-start | bytes 6916
  19.8 43.2 %copy-start.86 = (f32[2,3,96]{2,1,0:T(4,128)}, f32[2,3,96]{2,1,0:T(4,128)S(1)}, u32[]{:S(2)}) copy-start(f32[2,3,96]{2,1,0:T(4,128)S(1)} %copy.163) | copy-start | bytes 6916
  19.8 43.2 %copy-start.88 = (f32[2,3,96]{2,1,0:T(4,128)}, f32[2,3,96]{2,1,0:T(4,128)S(1)}, u32[]{:S(2)}) copy-start(f32[2,3,96]{2,1,0:T(4,128)S(1)} %copy.162) | copy-start | bytes 6916
  19.9 43.2 %copy-start.80 = (f32[2,3,96]{2,1,0:T(4,128)}, f32[2,3,96]{2,1,0:T(4,128)S(1)}, u32[]{:S(2)}) copy-start(f32[2,3,96]{2,1,0:T(4,128)S(1)} %copy.161) | copy-start | bytes 6916
  19.9 43.2 %copy-start.68 = (f32[2,3,96]{2,1,0:T(4,128)}, f32[2,3,96]{2,1,0:T(4,128)S(1)}, u32[]{:S(2)}) copy-start(f32[2,3,96]{2,1,0:T(4,128)S(1)} %copy.160) | copy-start | bytes 6916
  19.9 43.1 %copy-start.64 = (f32[2,3,96]{2,1,0:T(4,128)}, f32[2,3,96]{2,1,0:T(4,128)S(1)}, u32[]{:S(2)}) copy-start(f32[2,3,96]{2,1,0:T(4,128)S(1)} %copy.159) | copy-start | bytes 6916
  50.4 132.7 %copy-start.15 = (bf16[2,392,2,96]{1,3,2,0:T(8,128)(2,1)}, bf16[2,392,2,96]{1,3,2,0:T(8,128)(2,1)S(1)}, u32[]{:S(2)}) copy-start(bf16[2,392,2,96]{1,3,2,0:T(8,128)(2,1)S(1)} %copy.190) | copy-start | bytes 903172
  59.2 36.7 %copy-start.8 = (f32[784,576]{1,0:T(8,128)}, f32[784,576]{1,0:T(8,128)S(1)}, u32[]{:S(2)}) copy-start(f32[784,576]{1,0:T(8,128)S(1)} %fusion.123) | copy-start | bytes 5419012
  98.4 98.5 %copy-start.17 = (bf16[2,392,2,1,96]{1,4,2,0,3:T(8,128)(2,1)}, bf16[2,392,2,1,96]{1,4,2,0,3:T(8,128)(2,1)S(1)}, u32[]{:S(2)}) copy-start(bf16[2,392,2,1,96]{1,4,2,0,3:T(8,128)(2,1)S(1)} %copy.246) | copy-start | bytes 903172
  147.8 35.4 %copy-start.19 = (bf16[2,392,2,1,96]{1,4,2,0,3:T(8,128)(2,1)S(1)}, bf16[2,392,2,1,96]{1,4,2,0,3:T(8,128)(2,1)}, u32[]{:S(2)}) copy-start(bf16[2,392,2,1,96]{1,4,2,0,3:T(8,128)(2,1)} %copy.247) | copy-start | bytes 903172
  245.7 2.9 collective-permute-start
  250.8 111.6 %all-gather.15.cloned.1.call-start = ((), (), s32[]{:S(2)}) async-start(), calls=%async_computation.3 | async-start | bytes 1536000 | tf_op jit(solution)/shard_map/all_gather | solution.py:221
  324.2 3.3 collective-permute-start.1
  331.1 444.8 %all-reduce.75.cloned.1.call-start = ((), (), s32[]{:S(2)}) async-start(), calls=%async_computation.4 | async-start | bytes 7077888 | tf_op jit(solution)/shard_map/psum | solution.py:262
  644.3 46.7 %copy-start.9 = (f32[784,576]{1,0:T(8,128)S(1)}, f32[784,576]{1,0:T(8,128)}, u32[]{:S(2)}) copy-start(f32[784,576]{1,0:T(8,128)} %copy-done.8) | copy-start | bytes 5419012
  692.9 39.1 %copy-start.33 = (bf16[200,768]{1,0:T(8,128)(2,1)S(1)}, bf16[200,768]{1,0:T(8,128)(2,1)}, u32[]{:S(2)}) copy-start(bf16[200,768]{1,0:T(8,128)(2,1)} %get-tuple-element.116) | copy-start | bytes 921604
  692.9 39.5 %copy-start.32 = (bf16[200,768]{1,0:T(8,128)(2,1)S(1)}, bf16[200,768]{1,0:T(8,128)(2,1)}, u32[]{:S(2)}) copy-start(bf16[200,768]{1,0:T(8,128)(2,1)} %get-tuple-element.115) | copy-start | bytes 921604
  692.9 40.0 %copy-start.52 = (f32[768]{0:T(1024)S(1)}, f32[768]{0:T(1024)}, u32[]{:S(2)}) copy-start(f32[768]{0:T(1024)} %param.21) | copy-start | bytes 9220
  693.0 40.0 %copy-start.55 = (f32[196]{0:T(256)S(1)}, f32[196]{0:T(256)}, u32[]{:S(2)}) copy-start(f32[196]{0:T(256)} %copy-done.54) | copy-start | bytes 2356
  693.0 41.0 %copy-start.111 = (f32[196]{0:T(256)S(1)}, f32[196]{0:T(256)}, u32[]{:S(2)}) copy-start(f32[196]{0:T(256)} %copy-done.110) | copy-start | bytes 2356
  693.0 41.5 %copy-start.14 = (f32[196,768]{1,0:T(8,128)S(1)}, f32[196,768]{1,0:T(8,128)}, u32[]{:S(2)}) copy-start(f32[196,768]{1,0:T(8,128)} %copy-done.13) | copy-start | bytes 1806340
  693.0 41.5 %copy-start.29 = (bf16[196,768]{1,0:T(8,128)(2,1)S(1)}, bf16[196,768]{1,0:T(8,128)(2,1)}, u32[]{:S(2)}) copy-start(bf16[196,768]{1,0:T(8,128)(2,1)} %param.38) | copy-start | bytes 903172
  694.7 37.3 %collective-permute-start.3 = (bf16[12,768]{1,0:T(8,128)(2,1)S(1)}, bf16[12,768]{1,0:T(8,128)(2,1)S(1)}, u32[]{:S(2)}, u32[]{:S(2)}) collective-permute-start(bf16[12,768]{1,0:T(8,128)(2,1)S(1)} %slice.299), channel_id=1, source_target_pairs={{0,1},{1,2},{2,3},{4,5},{5,6},{6,7},{8,9},{9,10},{10,11},{12,13},{... | collective-permute-start | bytes 55304
  697.1 35.4 %collective-permute-start.2 = (bf16[12,768]{1,0:T(8,128)(2,1)S(1)}, bf16[12,768]{1,0:T(8,128)(2,1)S(1)}, u32[]{:S(2)}, u32[]{:S(2)}) collective-permute-start(bf16[12,768]{1,0:T(8,128)(2,1)S(1)} %slice.298), channel_id=1, source_target_pairs={{0,1},{1,2},{2,3},{4,5},{5,6},{6,7},{8,9},{9,10},{10,11},{12,13},{... | collective-permute-start | bytes 55304
  (88 other events, 878.7 us)
Sparse Core Ops, SparseCore 0:
  12.9 33.9 all-gather.8
  48.5 30.3 all-gather.12
  250.9 31.3 all-gather.10
  331.2 31.1 all-gather.14
  691.1 73.8 all-reduce.74
where the time goes:
time: 801 us; the launch traced here: 791 us
  other arithmetic  254 us (32%)
  local copies, waits for them, and re-layouts  170 us (21%)
  blocking collectives  167 us (21%)
  matrix products  121 us (15%)
  waiting for transfers between devices  52.6 us (7%)
  between operations  17 us (2%)
  starting transfers between devices  8.04 us (1%)
    unnamed x3, blocking collectives  104 us
    reshape x1, local copies, waits for them, and re-layouts, rel_bias(): return total.reshape(clip_count, head_count, 392, 392)  49.6 us
    reduce_sum x4, other arithmetic, pool_grid(): padded[:, shift_t:shift_t + 8, shift_h:shift_h + 7, shift_w:shift_w + 7]  45.9 us
    psum x1, blocking collectives, on_device(): lax.psum((g_ln1_gain, g_ln1_bias, g_proj_bias, g_ln2_gain, g_ln2_bias, g_...  39.2 us
    mul x6, other arithmetic, pool_grid(): padded[:, shift_t:shift_t + 8, shift_h:shift_h + 7, shift_w:shift_w + 7]  36.7 us
    add x1, local copies, waits for them, and re-layouts, rel_bias(): along_t[..., :, None, None] + along_h[..., None, :, None]  35.3 us
    convert_element_type x1, other arithmetic, on_device(): pooled.reshape(clip_count, 392, head_count, 3, head_size).astype(b_type)  32.8 us
    reduce_sum x1, other arithmetic, rel_bias(): along_t[..., :, None, None] + along_h[..., None, :, None]  31.2 us
  transfers between devices with their start and end apart: 9, of which 4 were waited for; matrix products, arithmetic and copies ran while one was open for 33% of the time, Pallas kernels for 0%

commit v1 on v0

v1 whole, which is shorter than its diff:
```python
import functools

import jax
import jax.numpy as jnp
from jax import lax
from jax.experimental import pallas as pl
from jax.experimental.pallas import tpu as pltpu
from jax.sharding import PartitionSpec as P

f_type = jnp.float32
b_type = jnp.bfloat16
eps_norm = 1e-06
neg_large = -1000000000.0
clip_rows = 392
grid_rows = 448
slot_rows = 448
block_rows = 112
vmem_bytes = 56 * 1024 * 1024


def dot(a, b):
    return jnp.dot(a, b, preferred_element_type=f_type)


def dot_nt(a, b):
    return lax.dot_general(a, b, (((1,), (1,)), ((), ())), preferred_element_type=f_type)


def iota(shape, axis):
    return lax.broadcasted_iota(jnp.int32, shape, axis)


def one_hot(flag):
    return jnp.where(flag, 1.0, 0.0).astype(b_type)


def split(values):
    high = values.astype(b_type)
    return high, (values - high.astype(f_type)).astype(b_type)


def aligned(start, step):
    return pl.multiple_of(start, step)


def call(kernel, name, cost, results, scalars, arrays, scratch=(), after=()):
    def body(*refs):
        kept = refs[: len(scalars) + len(arrays)]
        kernel(*kept, *refs[len(kept) + len(after) :])

    single = not isinstance(results, tuple)
    shapes = (results,) if single else results
    outs = pl.pallas_call(
        body,
        out_shape=tuple(jax.ShapeDtypeStruct(shape, kind) for shape, kind in shapes),
        in_specs=[pl.BlockSpec(memory_space=pltpu.SMEM)] * len(scalars)
        + [pl.BlockSpec(memory_space=pltpu.VMEM)] * len(arrays)
        + [pl.BlockSpec(memory_space=pl.ANY)] * len(after),
        out_specs=tuple(pl.BlockSpec(memory_space=pltpu.VMEM) for _ in shapes),
        scratch_shapes=list(scratch),
        compiler_params=pltpu.CompilerParams(vmem_limit_bytes=vmem_bytes),
        cost_estimate=pl.CostEstimate(
            flops=int(cost * 1e9), bytes_accessed=int(cost * 3e6), transcendentals=0
        ),
        name=name,
    )(*scalars, *arrays, *after)
    return outs[0] if single else outs


def spread_matrix(start, count):
    row = iota((grid_rows, count), 0)
    place = row & 7
    return one_hot(
        ((row >> 3) * 7 + place - start == iota((grid_rows, count), 1)) & (place < 7)
    )


def gather_matrix(start, count):
    row = iota((count, grid_rows), 1)
    place = row & 7
    return one_hot(
        ((row >> 3) * 7 + place - start == iota((count, grid_rows), 0)) & (place < 7)
    )


def to_grid(seat, pieces):
    total = None
    for step, piece in enumerate(pieces):
        rows = piece.shape[0]
        part = dot(spread_matrix((seat ^ step) * rows, rows), piece[...])
        total = part if total is None else total + part
    return total.astype(b_type)


def row_coords(shape, axis):
    row = iota(shape, axis)
    line = row >> 3
    frame = (line * 37) >> 8
    return frame, line - frame * 7, row & 7


def coord_of(kind, coords):
    frame, line, place = coords
    return jnp.where(kind == 0, frame, jnp.where(kind == 1, line, place))


def query_mask():
    shape = (grid_rows, 192)
    column = iota(shape, 1)
    coord = coord_of(column >> 6, row_coords(shape, 0))
    return jnp.where(((column >> 3) & 7) == coord, 1.0, 0.0)


def key_matrix():
    shape = (192, grid_rows)
    column = iota(shape, 0)
    coord = coord_of(column >> 6, row_coords(shape, 1))
    return one_hot((column & 7) == coord)


def table_slot(column):
    kind = column >> 6
    at_query = (column >> 3) & 7
    at_key = column & 7
    base = jnp.where(kind == 0, 7, jnp.where(kind == 1, 21, 34))
    valid = (kind == 0) | ((at_query < 7) & (at_key < 7))
    return jnp.where(valid, base + at_query - at_key, -1)


def table_matrix():
    return one_hot(table_slot(iota((192, 41), 0)) == iota((192, 41), 1))


def key_bias(limit):
    lane = iota((1, grid_rows), 1)
    own = jnp.where((lane & 7) == 7, neg_large, 0.0)
    group = jnp.zeros_like(lane)
    for step in range(1, 8):
        group = group + jnp.where(lane >= 56 * step, 1, 0)
    place = lane - 56 * group
    valid = (place < 49) & ((group & 3) < limit)
    return own, jnp.where(valid, 0.0, neg_large)


def clear_border(field):
    width = field.shape[-1]
    field[:, 0:1] = jnp.zeros((3, 1, 9, 8, width), f_type)
    field[:, 9:10] = jnp.zeros((3, 1, 9, 8, width), f_type)
    field[:, :, 0:1] = jnp.zeros((3, 10, 1, 8, width), f_type)
    field[:, :, 8:9] = jnp.zeros((3, 10, 1, 8, width), f_type)


def fill_field(field, values):
    width = values.shape[-1]
    lines = values.reshape(56, 8, width)
    field[0, 1:9, 1:8] = pltpu.roll(lines, 1, 1).reshape(8, 7, 8, width)
    field[1, 1:9, 1:8] = lines.reshape(8, 7, 8, width)
    field[2, 1:9, 1:8] = pltpu.roll(lines, 7, 1).reshape(8, 7, 8, width)


def convolve(field, taps, result, flip):
    width = field.shape[-1]
    for start in range(0, width, 128):
        lanes = slice(start, min(start + 128, width))

        def frame(t, carry):
            total = jnp.zeros((7, 8, lanes.stop - lanes.start), f_type)
            for dt in range(3):
                for dw in range(3):
                    near = field[dw, t + dt, :, :, lanes]
                    for dh in range(3):
                        tap = dt * 9 + dh * 3 + dw
                        tap = 26 - tap if flip else tap
                        total = total + near[dh : dh + 7] * taps[tap : tap + 1, lanes]
            result[t, :, :, lanes] = total
            return carry

        lax.fori_loop(0, 8, frame, 0)


def tap_grads(field, grads, result):
    width = field.shape[-1]
    for start in range(0, width, 128):
        lanes = slice(start, min(start + 128, width))
        size = lanes.stop - lanes.start

        def frame(t, sums):
            grad = grads[1, t + 1, 1:8, :, lanes]
            sums = list(sums)
            for dt in range(3):
                for dw in range(3):
                    near = field[dw, t + dt, :, :, lanes]
                    for dh in range(3):
                        tap = dt * 9 + dh * 3 + dw
                        sums[tap] = sums[tap] + jnp.sum(near[dh : dh + 7] * grad, axis=0)
            return tuple(sums)

        sums = lax.fori_loop(
            0, 8, frame, tuple(jnp.zeros((8, size), f_type) for _ in range(27))
        )
        for tap in range(27):
            result[tap : tap + 1, lanes] = jnp.sum(sums[tap], axis=0, keepdims=True)


class Rows:
    def __init__(self, heads, units, width):
        self.taps = 0
        self.table = self.taps + 96 * heads
        self.bias = self.table + 48 * heads
        self.weights = self.bias + 8
        self.comp = self.weights
        self.sums = self.comp + 16 * heads
        self.total = self.sums + 48
        self.units = units // 128
        self.width = width // 128


def wide_row(ref, start, count):
    return jnp.concatenate([ref[start + k : start + k + 1, :] for k in range(count)], axis=1)


def put_row(ref, start, values):
    for k in range(values.shape[1] // 128):
        ref[start + k : start + k + 1, :] = values[:, 128 * k : 128 * k + 128]


def vector(ref):
    return wide_row(ref, 0, ref.shape[0])


def seat_of(place, half):
    return place[0] & (half - 1)


def clip_of(place, half):
    return place[0] >> (half.bit_length() - 1)


def core_of(place):
    return place[1] & 1


def put_halves(whole, place, halves):
    size = halves[0].shape[0]
    for step, item in enumerate(halves):
        whole[pl.ds(aligned((core_of(place) ^ step) * size, size), size), :] = item[...]


def weight_views(refs, width):
    if len(refs) == 2:
        return refs[0], refs[1]
    return refs[0].at[0 : 3 * width], refs[0].at[3 * width : 4 * width]


def load_taps(taps, small, heads, size):
    for index in range(3 * heads):
        taps[0:27, index * size : (index + 1) * size] = small[
            32 * index : 32 * index + 27, 0:size
        ]


def attend_kernel(rows, heads, size, half, far, *refs):
    refs = list(refs)

    def take(count):
        found = refs[:count]
        del refs[:count]
        return found

    place, groups = take(2)
    pieces = take(half)
    chunks = take(2)
    small, mem = take(2)
    base = take(1)[0] if far else None
    if far:
        mine_ref, other_ref, all_weights = take(3)
    else:
        (branch_ref,) = take(1)
    pooled_ref, probs_ref, head_ref = take(3)
    field, taps, pooled_wide, head_wide, rel_high, rel_low = refs
    width = heads * size
    scale = size ** (-0.5)
    seat = seat_of(place, half)
    if far:
        put_halves(all_weights, place, chunks)
        chunks = [all_weights]
    w_qkv, w_proj = weight_views(chunks, width)
    clear_border(field)
    load_taps(taps, small, heads, size)
    fill_field(field, dot_nt(to_grid(seat, pieces), w_qkv[...]))
    convolve(field, taps, pooled_wide, False)
    pooled = pooled_wide[...].reshape(grid_rows, 3 * width)
    filled = (iota((grid_rows, 1), 0) & 7) < 7
    pooled_ref[...] = jnp.where(filled, pooled, 0.0).astype(b_type)
    own_bias, mem_bias = key_bias(4 >> groups[clip_of(place, half)])
    expand = table_matrix()
    keys_at = key_matrix()
    mask = query_mask()
    for head in range(heads):
        at = 3 * head * size
        lanes = slice(head * size, (head + 1) * size)
        queries = pooled_ref[:, at : at + size]
        keys = pooled_ref[:, at + size : at + 2 * size]
        values = pooled_ref[:, at + 2 * size : at + 3 * size]
        mem_keys = mem[0, lanes, :]
        mem_values = mem[1, lanes, :]
        start = rows.table + 48 * head
        table_high, table_low = split(small[start : start + 41, 0:size])
        rel = dot_nt(queries, dot(expand, table_high).astype(b_type)) + dot_nt(
            queries, dot(expand, table_low).astype(b_type)
        )
        high, low = split(rel * mask)
        rel_high[...] = high
        rel_low[...] = low

        def rows_step(step, carry, at=at, lanes=lanes, head=head, keys=keys, values=values,
                      mem_keys=mem_keys, mem_values=mem_values):
            block_at = pl.ds(aligned(step * block_rows, block_rows), block_rows)
            block = pooled_ref[block_at, at : at + size]
            own = (
                dot_nt(block, keys) * scale
                + (dot(rel_high[block_at, :], keys_at) + dot(rel_low[block_at, :], keys_at))
                + own_bias
            )
            mem = dot(block, mem_keys) * scale + mem_bias
            top = jnp.maximum(
                jnp.max(own, axis=-1, keepdims=True), jnp.max(mem, axis=-1, keepdims=True)
            )
            own = jnp.exp(own - top)
            mem = jnp.exp(mem - top)
            total = jnp.sum(own, axis=-1, keepdims=True) + jnp.sum(mem, axis=-1, keepdims=True)
            inverse = 1.0 / total
            own = own * inverse
            mem = mem * inverse
            probs_ref[head, 0, block_at, :] = own
            probs_ref[head, 1, block_at, :] = mem
            attended = dot(own.astype(b_type), values) + dot_nt(mem.astype(b_type), mem_values)
            head_wide[block_at, lanes] = attended + block.astype(f_type)
            return carry

        lax.fori_loop(0, grid_rows // block_rows, rows_step, 0)
    head_ref[...] = head_wide[...].astype(b_type)
    count = pieces[0].shape[0]
    for step in range(half):
        head_out = dot(gather_matrix((seat ^ step) * count, count), head_ref[...]).astype(b_type)
        part = dot(head_out, w_proj[...])
        if not far:
            branch_ref[step] = part
        elif step == 0:
            mine_ref[...] = part + base[0]
        else:
            other_ref[step - 1] = (part + base[step]).astype(b_type)


def attend(rows, heads, size, place, groups, pieces, weights, small, mem, base=None, after=()):
    width = heads * size
    half = len(pieces)
    count, model = pieces[0].shape
    far = base is not None
    branch = (
        (((count, model), f_type), ((half - 1, count, model), b_type), ((4 * width, model), b_type))
        if far
        else (((half, count, model), f_type),)
    )
    return call(
        functools.partial(attend_kernel, rows, heads, size, half, far),
        "attend",
        16,
        branch
        + (
            ((grid_rows, 3 * width), b_type),
            ((heads, 2, grid_rows, grid_rows), f_type),
            ((grid_rows, width), b_type),
        ),
        (place, groups),
        (*pieces, *weights, small, mem) + ((base,) if far else ()),
        scratch=(
            pltpu.VMEM((3, 10, 9, 8, 3 * width), f_type),
            pltpu.VMEM((32, 3 * width), f_type),
            pltpu.VMEM((8, 7, 8, 3 * width), f_type),
            pltpu.VMEM((grid_rows, width), f_type),
            pltpu.VMEM((grid_rows, 192), b_type),
            pltpu.VMEM((grid_rows, 192), b_type),
        ),
        after=after,
    )


def scores_back_kernel(rows, heads, size, half, parts, *refs):
    place = refs[0]
    pieces = refs[1 : 1 + half]
    weights = refs[1 + half : 1 + half + parts]
    (
        small, mem, pooled_ref, probs_ref, head_ref,
        d_pooled, d_mem_ref, d_table_ref, d_proj_ref,
        d_head_ref, d_low_ref, probs_low, d_scores, d_query,
    ) = refs[1 + half + parts :]
    width = heads * size
    scale = size ** (-0.5)
    w_proj = weight_views(weights, width)[1]
    d_branch = to_grid(seat_of(place, half), pieces)
    d_head = dot_nt(d_branch, w_proj[...])
    d_head_ref[...] = d_head
    d_low_ref[...] = d_head.astype(b_type)
    expand = table_matrix()
    keys_at = key_matrix()
    mask = query_mask()
    for head in range(heads):
        at = 3 * head * size
        lanes = slice(head * size, (head + 1) * size)
        queries = pooled_ref[:, at : at + size]
        keys = pooled_ref[:, at + size : at + 2 * size]
        values = pooled_ref[:, at + 2 * size : at + 3 * size]
        mem_keys = mem[0, lanes, :]
        mem_values = mem[1, lanes, :]

        def rows_step(step, carry, lanes=lanes, head=head, keys=keys, values=values,
                      mem_keys=mem_keys, mem_values=mem_values):
            block_at = pl.ds(aligned(step * block_rows, block_rows), block_rows)
            d_att = d_low_ref[block_at, lanes]
            own = probs_ref[head, 0, block_at, :]
            mem = probs_ref[head, 1, block_at, :]
            d_own = dot_nt(d_att, values)
            d_mem = dot(d_att, mem_values)
            inner = jnp.sum(own * d_own, axis=-1, keepdims=True) + jnp.sum(
                mem * d_mem, axis=-1, keepdims=True
            )
            d_own = (own * (d_own - inner)).astype(b_type)
            d_mem = (mem * (d_mem - inner)).astype(b_type)
            probs_low[0, block_at, :] = own.astype(b_type)
            probs_low[1, block_at, :] = mem.astype(b_type)
            d_scores[0, block_at, :] = d_own
            d_scores[1, block_at, :] = d_mem
            d_query[block_at, :] = (dot(d_own, keys) + dot_nt(d_mem, mem_keys)) * scale
            return carry

        lax.fori_loop(0, grid_rows // block_rows, rows_step, 0)
        start = rows.table + 48 * head
        table_high, table_low = split(small[start : start + 41, 0:size])
        rel_high, rel_low = split(dot_nt(d_scores[0], keys_at) * mask)
        wide_high = dot(expand, table_high).astype(b_type)
        wide_low = dot(expand, table_low).astype(b_type)
        d_rel = dot(rel_high, wide_high) + dot(rel_low, wide_high) + dot(rel_high, wide_low)
        d_pooled[:, at : at + size] = d_query[...] + d_head_ref[:, lanes] + d_rel
        queries_t = jnp.transpose(queries.astype(f_type)).astype(b_type)
        d_att_t = jnp.transpose(d_head_ref[:, lanes]).astype(b_type)
        wide_high, wide_low = split(dot(queries_t, rel_high) + dot(queries_t, rel_low))
        d_table = dot(wide_high, expand) + dot(wide_low, expand)
        d_table_ref[48 * head : 48 * head + 41, 0:size] = jnp.transpose(d_table)
        d_pooled[:, at + size : at + 2 * size] = jnp.transpose(dot(queries_t, d_scores[0])) * scale
        d_mem_ref[0, lanes, :] = (dot(queries_t, d_scores[1]) * scale).astype(b_type)
        d_pooled[:, at + 2 * size : at + 3 * size] = jnp.transpose(dot(d_att_t, probs_low[0]))
        d_mem_ref[1, lanes, :] = dot(d_att_t, probs_low[1]).astype(b_type)
    head_t = jnp.transpose(head_ref[...].astype(f_type)).astype(b_type)
    d_proj_ref[...] = dot(head_t, d_branch).astype(b_type)


def scores_back(rows, heads, size, place, pieces, weights, small, mem, pooled, probs, head, after=()):
    width = heads * size
    return call(
        functools.partial(scores_back_kernel, rows, heads, size, len(pieces), len(weights)),
        "scores_back",
        13,
        (
            ((grid_rows, 3 * width), f_type),
            ((2, width, slot_rows), b_type),
            ((48 * heads, 128), f_type),
            ((width, pieces[0].shape[1]), b_type),
        ),
        (place,),
        (*pieces, *weights, small, mem, pooled, probs, head),
        scratch=(
            pltpu.VMEM((grid_rows, width), f_type),
            pltpu.VMEM((grid_rows, width), b_type),
            pltpu.VMEM((2, grid_rows, grid_rows), b_type),
            pltpu.VMEM((2, grid_rows, grid_rows), b_type),
            pltpu.VMEM((grid_rows, size), f_type),
        ),
        after=after,
    )


def pool_back_kernel(rows, heads, size, half, parts, last, *refs):
    place = refs[0]
    pieces = refs[1 : 1 + half]
    weights = refs[1 + half : 1 + half + parts]
    refs = list(refs[1 + half + parts :])
    small, d_pooled, d_table, d_proj, d_bias = refs[:5]
    del refs[:5]
    base = refs.pop(0) if last else None
    if last:
        mine_ref, other_ref = refs.pop(0), refs.pop(0)
    else:
        norm_ref = refs.pop(0)
    keep_ref, send_ref, small_ref, field, grads, taps, wide, packed, d_taps = refs
    width = heads * size
    seat = seat_of(place, half)
    w_qkv = weight_views(weights, width)[0]
    clear_border(field)
    clear_border(grads)
    load_taps(taps, small, heads, size)
    tokens = to_grid(seat, pieces)
    fill_field(field, dot_nt(tokens, w_qkv[...]))
    fill_field(grads, d_pooled[...])
    convolve(grads, taps, wide, True)
    d_qkv = wide[...].reshape(grid_rows, 3 * width)
    low = d_qkv.astype(b_type)
    count = pieces[0].shape[0]
    for step in range(half):
        part = dot(gather_matrix((seat ^ step) * count, count), low).astype(b_type)
        part = dot(part, w_qkv[...])
        if not last:
            norm_ref[step] = part
        elif step == 0:
            mine_ref[...] = part + base[0]
        else:
            other_ref[step - 1] = (part + base[step]).astype(b_type)
    packed[0 : 3 * width, :] = dot(jnp.transpose(d_qkv).astype(b_type), tokens).astype(b_type)
    packed[3 * width : 4 * width, :] = d_proj[...]
    core = core_of(place)
    keep_ref[...] = packed[pl.ds(aligned(core * (2 * width), 2 * width), 2 * width), :]
    send_ref[...] = packed[pl.ds(aligned((1 - core) * (2 * width), 2 * width), 2 * width), :]
    tap_grads(field, grads, d_taps)
    for index in range(3 * heads):
        small_ref[32 * index : 32 * index + 27, 0:size] = d_taps[
            0:27, index * size : (index + 1) * size
        ]
    small_ref[rows.table : rows.table + 48 * heads, :] = d_table[...]
    small_ref[rows.bias : rows.bias + 8, :] = d_bias[...]


def pool_back(rows, heads, size, place, pieces, weights, small, d_pooled, d_table, d_proj, d_bias,
              base=None, after=()):
    width = heads * size
    half = len(pieces)
    count, model = pieces[0].shape
    last = base is not None
    norm = (
        (((count, model), f_type), ((half - 1, count, model), b_type))
        if last
        else (((half, count, model), f_type),)
    )
    return call(
        functools.partial(pool_back_kernel, rows, heads, size, half, len(weights), last),
        "pool_back",
        9,
        norm
        + (
            ((2 * width, model), b_type),
            ((2 * width, model), b_type),
            ((rows.weights, 128), f_type),
        ),
        (place,),
        (*pieces, *weights, small, d_pooled, d_table, d_proj, d_bias) + ((base,) if last else ()),
        scratch=(
            pltpu.VMEM((3, 10, 9, 8, 3 * width), f_type),
            pltpu.VMEM((3, 10, 9, 8, 3 * width), f_type),
            pltpu.VMEM((32, 3 * width), f_type),
            pltpu.VMEM((8, 7, 8, 3 * width), f_type),
            pltpu.VMEM((4 * width, model), b_type),
            pltpu.VMEM((32, 3 * width), f_type),
        ),
        after=after,
    )


def frame_of(token):
    return (token * 669) >> 15


def tap_matrix(group):
    frame = frame_of(iota((8, clip_rows), 1))
    return one_hot((frame & ((2 << group) - 1)) == iota((8, clip_rows), 0))


def slot_matrix(which, group):
    token = iota((clip_rows, slot_rows), 0)
    slot = iota((clip_rows, slot_rows), 1)
    frame = frame_of(token)
    line = (slot * 586) >> 15
    return one_hot(
        ((line >> 2) == which)
        & ((line & 3) == (frame >> (group + 1)))
        & (slot - 56 * line == token - 49 * frame)
    )


def compress_kernel(half, other, place, rows_ref, groups, bank_a, bank_b, taps_ref, out_ref):
    group = groups[clip_of(place, half) ^ other]
    spread = tap_matrix(group)
    slots = [slot_matrix(which, group) for which in range(2)]
    for kind in range(2):
        high, low = split(taps_ref[kind])
        factor = dot(high, spread) + dot(low, spread)
        total = None
        for which, bank in enumerate((bank_a, bank_b)):
            high, low = split(bank[0, kind].astype(f_type) * factor)
            part = dot(high, slots[which]) + dot(low, slots[which])
            total = part if total is None else total + part
        out_ref[kind] = total.astype(b_type)


def bank_spec(width, half, other, which):
    def where(step, place, rows_ref, groups):
        return rows_ref[clip_of(place, half) ^ other, which], 0, 0, 0

    return pl.BlockSpec((1, 2, width, clip_rows), where)


def whole_spec(shape):
    return pl.BlockSpec(shape, lambda *_: (0,) * len(shape))


def compress(half, scalars, bank, taps, other):
    width = bank.shape[2]
    return pl.pallas_call(
        functools.partial(compress_kernel, half, other),
        out_shape=jax.ShapeDtypeStruct((2, width, slot_rows), b_type),
        grid_spec=pltpu.PrefetchScalarGridSpec(
            num_scalar_prefetch=3,
            grid=(1,),
            in_specs=[bank_spec(width, half, other, which) for which in range(2)]
            + [whole_spec((2, width, 8))],
            out_specs=whole_spec((2, width, slot_rows)),
        ),
        compiler_params=pltpu.CompilerParams(vmem_limit_bytes=vmem_bytes),
        cost_estimate=pl.CostEstimate(flops=3 * 10**9, bytes_accessed=10**7, transcendentals=0),
        name="compress",
    )(*scalars, bank, bank, taps)


def compress_back_kernel(half, place, rows_ref, groups, *refs):
    banks, grads, out_ref = refs[:4], refs[4:6], refs[6]
    totals = [None, None]
    for other in range(2):
        group = groups[clip_of(place, half) ^ other]
        taps = tap_matrix(group)
        for which in range(2):
            slots = slot_matrix(which, group)
            for kind in range(2):
                bank = banks[2 * other + which][0, kind].astype(f_type)
                high, low = split(bank * dot_nt(grads[other][kind], slots))
                part = dot_nt(taps, high) + dot_nt(taps, low)
                totals[kind] = part if totals[kind] is None else totals[kind] + part
    for kind in range(2):
        out_ref[kind] = totals[kind]


def compress_back(half, scalars, bank, grad_here, grad_other):
    width = bank.shape[2]
    return pl.pallas_call(
        functools.partial(compress_back_kernel, half),
        out_shape=jax.ShapeDtypeStruct((2, 8, width), f_type),
        grid_spec=pltpu.PrefetchScalarGridSpec(
            num_scalar_prefetch=3,
            grid=(1,),
            in_specs=[
                bank_spec(width, half, other, which) for other in range(2) for which in range(2)
            ]
            + [whole_spec((2, width, slot_rows))] * 2,
            out_specs=whole_spec((2, 8, width)),
        ),
        compiler_params=pltpu.CompilerParams(vmem_limit_bytes=vmem_bytes),
        cost_estimate=pl.CostEstimate(flops=5 * 10**9, bytes_accessed=10**7, transcendentals=0),
        name="compress_back",
    )(*scalars, bank, bank, bank, bank, grad_here, grad_other)


def normal_rows(values):
    centered = values - jnp.mean(values, axis=-1, keepdims=True)
    inverse = lax.rsqrt(jnp.mean(centered * centered, axis=-1, keepdims=True) + eps_norm)
    return centered * inverse, inverse


def norm_back(normal, inverse, grad, gain):
    scaled = grad * gain
    return inverse * (
        scaled
        - jnp.mean(scaled, axis=-1, keepdims=True)
        - normal * jnp.mean(scaled * normal, axis=-1, keepdims=True)
    )


def column_sum(values):
    return jnp.sum(values, axis=0, keepdims=True)


def add_pieces(mine, others):
    total = mine[...]
    for other in others:
        total = total + other[0].astype(f_type)
    return total


def open_kernel(rows, heads, size, rows_ref, gain, shift, pool, table, bias, out_ref, small):
    normal, _ = normal_rows(rows_ref[...].astype(f_type))
    out_ref[...] = (normal * vector(gain) + vector(shift)).astype(b_type)
    for head in range(heads):
        for part in range(3):
            start = 32 * (3 * head + part)
            for tap in range(27):
                small[start + tap : start + tap + 1, 0:size] = pool[part, tap, head : head + 1, :]
        start = rows.table + 48 * head
        for slot in range(41):
            small[start + slot : start + slot + 1, 0:size] = table[slot, head : head + 1, :]
    small[rows.bias : rows.bias + rows.units, :] = bias[...]


def second_norm_kernel(half, rows_ref, mine, *refs):
    others = refs[: half - 1]
    bias, gain, shift, mid_ref, out_ref = refs[half - 1 :]
    midway = rows_ref[...].astype(f_type) + (add_pieces(mine, others) + vector(bias))
    mid_ref[...] = midway
    normal, _ = normal_rows(midway)
    out_ref[...] = (normal * vector(gain) + vector(shift)).astype(b_type)


def second_back_kernel(half, mid_ref, mine, *refs):
    others = refs[: half - 1]
    top_ref, gain, d_mid_ref, d_low_ref, sums_ref = refs[half - 1 :]
    normal, inverse = normal_rows(mid_ref[...])
    grad = add_pieces(mine, others)
    top = top_ref[...].astype(f_type)
    d_mid = top + norm_back(normal, inverse, grad, vector(gain))
    d_mid_ref[...] = d_mid
    d_low = d_mid.astype(b_type)
    d_low_ref[...] = d_low
    put_row(sums_ref, 0, column_sum(d_low.astype(f_type)))
    put_row(sums_ref, 8, column_sum(grad * normal))
    put_row(sums_ref, 16, column_sum(grad))
    put_row(sums_ref, 24, column_sum(top))


def first_back_kernel(rows, heads, size, half, rows_ref, d_mid_ref, gain, mine, *refs):
    others = refs[: half - 1]
    refs = refs[half - 1 :]
    mid_ref, down_bias, mlp_mine = refs[:3]
    mlp_others = refs[3 : 2 + half]
    small_a, small_b, comp, sums, out_ref, y_ref, late = refs[2 + half :]
    normal, inverse = normal_rows(rows_ref[...].astype(f_type))
    grad = add_pieces(mine, others)
    out_ref[...] = d_mid_ref[...] + norm_back(normal, inverse, grad, vector(gain))
    y_ref[...] = (mid_ref[...] + add_pieces(mlp_mine, mlp_others) + vector(down_bias)).astype(b_type)
    late[0 : rows.weights, :] = small_a[...] + small_b[...]
    for head in range(heads):
        for part in range(2):
            start = rows.comp + 8 * (2 * head + part)
            late[start : start + 8, 0:size] = comp[part, :, head * size : (head + 1) * size]
    late[rows.sums : rows.sums + 32, :] = sums[...]
    put_row(late, rows.sums + 32, column_sum(grad * normal))
    put_row(late, rows.sums + 40, column_sum(grad))


def close_kernel(rows, heads, size, late, *refs):
    pool, table, comp, bias = refs[:4]
    for head in range(heads):
        for part in range(3):
            start = 32 * (3 * head + part)
            for tap in range(27):
                pool[part, tap, head : head + 1, :] = late[start + tap : start + tap + 1, 0:size]
        start = rows.table + 48 * head
        for slot in range(41):
            table[slot, head : head + 1, :] = late[start + slot : start + slot + 1, 0:size]
        for part in range(2):
            start = rows.comp + 8 * (2 * head + part)
            comp[head, part] = late[start : start + 8, 0:size]
    bias[...] = late[rows.bias : rows.bias + rows.units, :]


def error_function(values):
    x = jnp.clip(values, -4.0, 4.0)
    y = x * x
    top = -2.72614225801306e-10
    for term in (
        2.77068142495902e-08,
        -2.10102402082508e-06,
        -5.69250639462346e-05,
        -7.34990630326855e-04,
        -2.95459980854025e-03,
        -1.60960333262415e-02,
    ):
        top = top * y + term
    low = -1.45660718464996e-05
    for term in (
        -2.13374055278905e-04,
        -1.68282697438203e-03,
        -7.37332916720468e-03,
        -1.42647390514189e-02,
    ):
        low = low * y + term
    return x * top / low


def mlp_kernel(rows, half, flip, part, place, *refs):
    pieces, tops = refs[:half], refs[half : 2 * half]
    refs = refs[2 * half :]
    up, down = refs[:2]
    halves = refs[2:4]
    (
        bias, small, y_mine, y_other, d_mine, d_other,
        left_keep, right_keep, left_send, right_send, sums,
        tokens_all, top_all, far, y_all, d_all,
    ) = refs[4:]
    put_halves(far, place, halves)
    ups = halves[0].shape[0]
    count = pieces[0].shape[0]
    tokens = jnp.concatenate([piece[...].astype(f_type) for piece in pieces], axis=0).astype(b_type)
    top = jnp.concatenate([piece[...].astype(f_type) for piece in tops], axis=0).astype(b_type)
    units = down.shape[0]
    y_all[...] = jnp.zeros(y_all.shape, f_type)
    d_all[...] = jnp.zeros(d_all.shape, f_type)
    even = core_of(place) == 0
    for block in range(2):
        first = up if block == 0 else far.at[0:ups]
        second = down if block == 0 else far.at[ups : 2 * ups]
        shift = wide_row(bias, 0, rows.units) if block == 0 else wide_row(small, rows.bias, rows.units)
        for start in range(0, units, part):
            here = slice(start, start + part)
            if flip:
                hidden = dot_nt(tokens, first[here, :]) + shift[:, here]
            else:
                hidden = dot(tokens, first[:, here]) + shift[:, here]
            half_slope = 0.5 * (1.0 + error_function(hidden * (0.5**0.5)))
            slope = half_slope + hidden * jnp.exp(-0.5 * hidden * hidden) * 0.3989422804014327
            act = (hidden * half_slope).astype(b_type)
            d_hid = (dot_nt(top, second[here, :]) * slope).astype(b_type)
            put_row(sums, 8 * block + start // 128, column_sum(d_hid.astype(f_type)))
            y_all[...] += dot(act, second[here, :])
            if flip:
                d_all[...] += dot(d_hid, first[here, :])
            else:
                d_all[...] += dot_nt(d_hid, first[:, here])

            def store(keep, send, here=here, act=act, d_hid=d_hid, block=block):
                keep[0 if flip else 1][block, :, here] = d_hid
                send[0][block, :, here] = act

            @pl.when(even)
            def _():
                store((left_keep, right_keep), (left_send, right_send))

            @pl.when(jnp.logical_not(even))
            def _():
                store((left_send, right_send), (left_keep, right_keep))

        def fixed(keep, send, block=block):
            keep[1 if flip else 0][block] = tokens
            send[1][block] = top

        @pl.when(even)
        def _():
            fixed((left_keep, right_keep), (left_send, right_send))

        @pl.when(jnp.logical_not(even))
        def _():
            fixed((left_send, right_send), (left_keep, right_keep))

    y_mine[...] = y_all[0:count, :]
    d_mine[...] = d_all[0:count, :]
    for step in range(1, half):
        span = slice(step * count, (step + 1) * count)
        y_other[step - 1] = y_all[span, :].astype(b_type)
        d_other[step - 1] = d_all[span, :].astype(b_type)


def mlp(rows, flip, place, pieces, tops, up, down, chunks, bias, small, after=()):
    half = len(pieces)
    count, model = pieces[0].shape
    total = half * count
    units = down.shape[0]
    part = 256 if units % 256 == 0 else units
    left = ((2, total, units if flip else model), b_type)
    down_left = ((2, total, units), b_type)
    right = ((2, total, model), b_type)
    assert left == down_left
    return call(
        functools.partial(mlp_kernel, rows, half, flip, part),
        "mlp",
        12,
        (
            ((count, model), f_type),
            ((half - 1, count, model), b_type),
            ((count, model), f_type),
            ((half - 1, count, model), b_type),
            left,
            right,
            left,
            right,
            ((16, 128), f_type),
        ),
        (place,),
        (*pieces, *tops, up, down, *chunks, bias, small),
        scratch=(
            pltpu.VMEM((total, model), b_type),
            pltpu.VMEM((total, model), b_type),
            pltpu.VMEM((2 * chunks[0].shape[0], model), b_type),
            pltpu.VMEM((total, model), f_type),
            pltpu.VMEM((total, model), f_type),
        ),
        after=after,
    )


def swap_pairs(count, bit):
    return [(place, place ^ bit) for place in range(count)]


class Team:
    def __init__(self, heads_count, clips_count):
        self.total = heads_count
        self.half = heads_count // 2
        self.clips = clips_count
        self.here = lax.axis_index("head")
        self.clip = self.here // self.half
        self.seat = self.here % self.half
        self.spot = lax.axis_index("clip")

    def partner(self, values):
        return lax.ppermute(values, "head", swap_pairs(self.total, self.half))

    def seats(self, values, step):
        return lax.ppermute(values, "head", swap_pairs(self.total, step))

    def swap(self, values, bit):
        return lax.ppermute(values, "clip", swap_pairs(self.clips, bit))

    def gather(self, rows):
        return [rows] + [self.seats(rows, step) for step in range(1, self.half)]

    def scatter(self, others):
        return [self.seats(others[step - 1 : step], step) for step in range(1, self.half)]

    def eighth(self):
        return (self.spot & 1) * 4 + self.seat_in((2, 4))

    def share(self, came):
        mine = self.collect(came, (2, 4))
        return [mine, self.swap(mine, 1)]

    def quads(self):
        bit, found = 2, []
        while bit < self.clips:
            found.append((bit, 2 * bit))
            bit *= 4
        return found

    def seat_in(self, quad):
        return (self.spot // quad[0]) % 2 + 2 * ((self.spot // quad[1]) % 2)

    def peer(self, values, quad, step):
        return self.swap(values, (step & 1) * quad[0] + (step >> 1) * quad[1])

    def cut(self, values, quad):
        size = values[0].shape[-2] // 4
        seat = self.seat_in(quad)

        def quarter(place):
            total = None
            for item in values:
                part = lax.dynamic_slice_in_dim(item, place * size, size, axis=-2).astype(f_type)
                total = part if total is None else total + part
            return total

        return [quarter(seat)] + [quarter(seat ^ step).astype(b_type) for step in (1, 2, 3)]

    def collect(self, chunk, quad):
        seat = self.seat_in(quad)
        pieces = [chunk] + [self.peer(chunk, quad, step) for step in (1, 2, 3)]
        return jnp.concatenate(
            [lax.select_n((seat ^ place).astype(jnp.int32), *pieces) for place in range(4)], axis=0
        )

    def reduce(self, keep, send):
        values, sent = [keep, self.swap(send, 1)], ()
        for quad in self.quads():
            values = self.cut(values, quad)
            sent = sent or tuple(values)
            values = [values[0]] + [self.peer(values[step], quad, step) for step in (1, 2, 3)]
        return values, sent

    def finish(self, chunk):
        for quad in reversed(self.quads()):
            chunk = self.collect(chunk, quad)
        other = self.swap(chunk, 1)
        odd = (self.spot & 1) != 0
        return jnp.where(odd, other, chunk), jnp.where(odd, chunk, other)


def add(values):
    total = values[0].astype(f_type)
    for item in values[1:]:
        total = total + item.astype(f_type)
    return total


def on_device(
    heads_total,
    clips_total,
    inputs,
    ln1_gain,
    ln1_bias,
    w_qkv,
    pool_kernel,
    rel_table,
    comp_kernel,
    memory_bank,
    mem_index,
    clip_group,
    w_proj,
    proj_bias,
    ln2_gain,
    ln2_bias,
    w_up,
    up_bias,
    w_down,
    down_bias,
    cotangent,
):
    team = Team(heads_total, clips_total)
    half = team.half
    heads, _, size = rel_table.shape
    count, model = inputs.shape
    units = w_up.shape[1]
    width = heads * size
    rows = Rows(heads, units, model)
    flip = units != model
    lined = [
        item.reshape(model // 128, 128)
        for item in (ln1_gain, ln1_bias, proj_bias, ln2_gain, ln2_bias, down_bias)
    ]
    gain1, shift1, bias_proj, gain2, shift2, bias_down = lined
    bias_up = up_bias.reshape(units // 128, 128)
    w_qkv = w_qkv.T
    if flip:
        w_up = w_up.T
    bank = memory_bank.transpose(0, 1, 3, 2)
    place = jnp.stack([team.here, team.spot])
    scalars = (place, mem_index, clip_group)

    norm1, small = call(
        functools.partial(open_kernel, rows, heads, size),
        "open",
        2,
        (((count, model), b_type), ((rows.weights, 128), f_type)),
        (),
        (
            inputs,
            gain1,
            shift1,
            pool_kernel.transpose(1, 2, 0, 3),
            rel_table.transpose(1, 0, 2),
            bias_up,
        ),
    )
    tokens1 = team.gather(norm1)
    eighth = team.eighth()
    part = width // 2
    chunk_a = jnp.where(
        eighth < 6,
        lax.dynamic_slice_in_dim(w_qkv, jnp.minimum(eighth, 5) * part, part, axis=0),
        lax.dynamic_slice_in_dim(w_proj, (eighth & 1) * part, part, axis=0),
    )
    part = units // 4
    chunk_b = jnp.where(
        eighth < 4,
        lax.dynamic_slice_in_dim(w_up, (eighth & 3) * part, part, axis=0),
        lax.dynamic_slice_in_dim(w_down, (eighth & 3) * part, part, axis=0),
    )
    came_a = team.partner(chunk_a)
    comp_taps = comp_kernel.transpose(1, 0, 3, 2).reshape(2, width, 8)
    mem_far = team.partner(compress(half, scalars, bank, comp_taps, 1))
    mem_here = compress(half, scalars, bank, comp_taps, 0)
    small_far = team.partner(small)
    came_b = team.partner(chunk_b)
    tops = team.gather(cotangent)
    chunks_a = team.share(came_a)
    chunks_b = team.share(came_b)

    weights_here = (w_qkv, w_proj)
    branch, pooled_here, probs_here, heads_here = attend(
        rows, heads, size, place, clip_group, tokens1, weights_here, small, mem_here,
        after=(came_a, chunk_b),
    )
    branch, branch_other, weights, pooled_far, probs_far, heads_far = attend(
        rows, heads, size, place, clip_group, tokens1, chunks_a, small_far, mem_far, base=branch,
        after=(*tops,),
    )
    weights_far = (weights,)
    branch_came = team.scatter(branch_other)
    midway, norm2 = call(
        functools.partial(second_norm_kernel, half),
        "second_norm",
        2,
        (((count, model), f_type), ((count, model), b_type)),
        (),
        (inputs, branch, *branch_came, bias_proj, gain2, shift2),
    )
    tokens2 = team.gather(norm2)
    y, y_other, d_norm2, d_norm2_other, left_k, right_k, left_s, right_s, d_bias = mlp(
        rows, flip, place, tokens2, tops, w_up, w_down, chunks_b, bias_up, small_far
    )
    d_norm2_came = team.scatter(d_norm2_other)
    y_came = team.scatter(y_other)

    def product(a, b):
        return lax.dot_general(
            a, b, (((1,), (1,)), ((0,), (0,))), preferred_element_type=f_type
        ).astype(b_type)

    send_m = product(left_s, right_s)
    keep_m = product(left_k, right_k)
    sums_m, sent_m = team.reduce(keep_m, send_m)
    d_mid, d_branch, sums2 = call(
        functools.partial(second_back_kernel, half),
        "second_back",
        3,
        (((count, model), f_type), ((count, model), b_type), ((32, 128), f_type)),
        (),
        (midway, d_norm2, *d_norm2_came, cotangent, gain2),
    )
    d_branches = team.gather(d_branch)

    d_pooled, d_mem_far, d_table, d_proj = scores_back(
        rows, heads, size, place, d_branches, weights_far, small_far, mem_far, pooled_far,
        probs_far, heads_far, after=(*sent_m, *y_came),
    )
    d_mem_back = team.partner(d_mem_far)
    d_norm1, keep_f, send_f, grads_far = pool_back(
        rows, heads, size, place, tokens1, weights_far, small_far, d_pooled, d_table, d_proj,
        d_bias[8:16],
    )
    sums_f, sent_f = team.reduce(keep_f, send_f)
    grads_came = team.partner(grads_far)
    sum_m = add(sums_m)
    part_m = sum_m[1].astype(b_type)
    chunk_m = (sum_m[0] + team.partner(part_m).astype(f_type)).astype(b_type)
    d_pooled, d_mem_here, d_table, d_proj = scores_back(
        rows, heads, size, place, d_branches, weights_here, small, mem_here, pooled_here,
        probs_here, heads_here, after=(d_norm1, part_m),
    )
    d_norm1, d_norm1_other, keep_o, send_o, grads_here = pool_back(
        rows, heads, size, place, tokens1, weights_here, small, d_pooled, d_table, d_proj,
        d_bias[0:8], base=d_norm1, after=(chunk_m, *sent_f, d_mem_back, grads_came),
    )
    d_norm1_came = team.scatter(d_norm1_other)
    g_up, g_down = team.finish(chunk_m)
    sums_o, _ = team.reduce(keep_o, send_o)
    came_f = team.partner(add(sums_f).astype(b_type))
    chunk_o = add([*sums_o, came_f]).astype(b_type)
    g_a, g_b = team.finish(chunk_o)
    g_comp = compress_back(half, scalars, bank, d_mem_here, d_mem_back)
    grad_inputs, output, late = call(
        functools.partial(first_back_kernel, rows, heads, size, half),
        "first_back",
        3,
        (((count, model), f_type), ((count, model), b_type), ((rows.total, 128), f_type)),
        (),
        (
            inputs, d_mid, gain1, d_norm1, *d_norm1_came, midway, bias_down, y, *y_came,
            grads_here, grads_came, g_comp, sums2,
        ),
    )
    late = late + team.swap(late, 1)
    for quad in team.quads():
        late = add([late] + [team.peer(late, quad, step) for step in (1, 2, 3)])
    sums = late[rows.sums :]
    sums = add([sums] + [team.seats(sums, step) for step in range(1, team.total)])
    g_pool, g_rel, g_comp, g_bias = call(
        functools.partial(close_kernel, rows, heads, size),
        "close",
        1,
        (
            ((3, 27, heads, size), f_type),
            ((41, heads, size), f_type),
            ((heads, 2, 8, size), f_type),
            ((units // 128, 128), f_type),
        ),
        (),
        (late,),
    )
    g_attn = jnp.concatenate([g_a, g_b], axis=0).astype(f_type)
    g_up, g_down = g_up.astype(f_type), g_down.astype(f_type)
    if flip:
        g_up = g_up.T

    def total(index):
        return sums[8 * index : 8 * index + model // 128].reshape(model)

    return (
        output,
        grad_inputs,
        total(4),
        total(5),
        g_attn[: 3 * width].T,
        g_pool.transpose(2, 0, 1, 3),
        g_rel.transpose(1, 0, 2),
        g_comp,
        g_attn[3 * width :],
        total(0),
        total(1),
        total(2),
        g_up,
        g_bias.reshape(units),
        g_down,
        total(3),
    )


def solution(mesh):
    return jax.shard_map(
        functools.partial(on_device, mesh.shape["head"], mesh.shape["clip"]),
        mesh=mesh,
        in_specs=(
            P(("clip", "head"), None),
            P(),
            P(),
            P(None, "head"),
            P("head", None, None, None),
            P("head", None, None),
            P("head", None, None, None),
            P("clip", None, None, "head"),
            P("clip", None),
            P("clip"),
            P("head", None),
            P(),
            P(),
            P(),
            P(None, "head"),
            P("head"),
            P("head", None),
            P(),
            P(("clip", "head"), None),
        ),
        out_specs=(
            P(("clip", "head"), None),
            P(("clip", "head"), None),
            P(),
            P(),
            P(None, "head"),
            P("head", None, None, None),
            P("head", None, None),
            P("head", None, None, None),
            P("head", None),
            P(),
            P(),
            P(),
            P(None, "head"),
            P("head"),
            P("head", None),
            P(),
        ),
        check_vma=False,
    )
```

time: 801 us -> 297 us (0.37)
  other arithmetic: 254 us -> 15.2 us
  blocking collectives: 167 us -> 0 us
  local copies, waits for them, and re-layouts: 170 us -> 10.4 us
  Pallas kernels: 0 us -> 124 us
  matrix products: 121 us -> 7.57 us
  starting transfers between devices: 8.04 us -> 59.2 us
  waiting for transfers between devices: 52.6 us -> 74 us
  between operations: 17 us -> 1.6 us
    pallas_call x0 -> x15, Pallas kernels: none -> 124 us  [the longest x12 110 us: call(): pl.pallas_call(body, out_shape=tuple((jax.ShapeDtypeStruct(shape, kind) f...]
    dot_general x32 -> x2, matrix products: 121 us -> 7.57 us  [product(): lax.dot_general(a, b, (((1,), (1,)), ((0,), (0,))), preferred_element_typ...]
    unnamed x3 -> x0, blocking collectives: 104 us -> none
    reduce_sum x16 -> x0, other arithmetic: 87 us -> none  [the longest x4 45.9 us: pool_grid(): padded[:, shift_t:shift_t + 8, shift_h:shift_h + 7, shift_w:shift_w + 7]]
    ppermute x0 -> x51, waiting for transfers between devices: none -> 74 us  [the longest x11 34.3 us: seats(): return lax.ppermute(values, 'head', swap_pairs(self.total, step))]
    psum x2 -> x0, blocking collectives: 63.5 us -> none  [the longest x1 39.2 us: on_device(): lax.psum((g_ln1_gain, g_ln1_bias, g_proj_bias, g_ln2_gain, g_ln2_bias, g_...]
    ppermute x0 -> x51, starting transfers between devices: none -> 59.2 us  [the longest x32 31.6 us: swap(): return lax.ppermute(values, 'clip', swap_pairs(self.clips, bit))]
    reshape x5 -> x1, local copies, waits for them, and re-layouts: 54.5 us -> 0.62 us  [total(): return sums[8 * index:8 * index + model // 128].reshape(model)]
  transfers between devices with their start and end apart: 9 -> 51, of which waited for: 4 -> 19; matrix products, arithmetic and copies ran while one was open for 33% -> 6% of each run, Pallas kernels for 0% -> 38%
where the time goes in v1:
time: 297 us; the launch traced here: 292 us
  Pallas kernels  124 us (42%)
  waiting for transfers between devices  74 us (25%)
  starting transfers between devices  59.2 us (20%)
  other arithmetic  15.2 us (5%)
  local copies, waits for them, and re-layouts  10.4 us (4%)
  matrix products  7.57 us (3%)
    pallas_call x12, Pallas kernels, call(): pl.pallas_call(body, out_shape=tuple((jax.ShapeDtypeStruct(shape, kind) f...  110 us
    ppermute x11, waiting for transfers between devices, seats(): return lax.ppermute(values, 'head', swap_pairs(self.total, step))  34.3 us
    ppermute x32, starting transfers between devices, swap(): return lax.ppermute(values, 'clip', swap_pairs(self.clips, bit))  31.6 us
    ppermute x32, waiting for transfers between devices, swap(): return lax.ppermute(values, 'clip', swap_pairs(self.clips, bit))  26.8 us
    ppermute x11, starting transfers between devices, seats(): return lax.ppermute(values, 'head', swap_pairs(self.total, step))  14.9 us
    ppermute x8, waiting for transfers between devices, partner(): return lax.ppermute(values, 'head', swap_pairs(self.total, self.half))  12.9 us
    ppermute x8, starting transfers between devices, partner(): return lax.ppermute(values, 'head', swap_pairs(self.total, self.half))  12.7 us
    pallas_call x2, Pallas kernels, compress(): pl.pallas_call(functools.partial(compress_kernel, half, other), out_shape...  8.28 us
  transfers between devices with their start and end apart: 51, of which 19 were waited for; matrix products, arithmetic and copies ran while one was open for 6% of the time, Pallas kernels for 38%

profile of v1, /device:TPU:0, one launch (start us, length us, event | category | flops | bytes accessed | tf_op | source)
XLA Modules:
  0.0 292.1 jit_solution(16796379834120493901)
XLA Ops:
  1.8 4.1 %collective-permute-start.11 = (bf16[192,768]{1,0:T(8,128)(2,1)S(1)}, bf16[192,768]{1,0:T(8,128)(2,1)S(1)}, u32[]{:S(2)}, u32[]{:S(2)}) collective-permute-start(bf16[192,768]{1,0:T(8,128)(2,1)S(1)} %dynamic-slice_select_fusion.refs_9_), channel_id=1, source_target_pairs={{0,2},{1,3},{2,0},{3,1},{4,6},{5,7},{6,4},{7,5},{8,10},{9,11},{10,... | collective-permute-start | bytes 884744 | tf_op jit(solution)/shard_map/ppermute | solution.py:919
  7.1 2.1 open.1
  9.2 1.9 collective-permute-start
  12.5 4.1 %compress.3.refs_7_.refs_6_ = bf16[2,192,448]{2,1,0:T(8,128)(2,1)} custom-call(s32[2]{0:T(128)} %pad_add_fusion.place.refs_0_, s32[2,2]{1,0:T(2,128)} %rows_ref.5, s32[2]{0:T(128)} %groups.5, bf16[8,2,192,392]{3,2,1,0:T(8,128)(2,1)} %bitcast.52, bf16[8,2,192,392]{3,2,1,0:T(8,128)(2,1)} %bitcast.53, f32[2,192,8]{2,1,0:T(8,128)} %bitcast.46), custom_call_target="tpu_custom_call" | custom-call | flops 3000000000 | bytes 10000000 | tf_op jit(solution)/shard_map/compress/pallas_call | solution.py:616
  16.6 9.1 %collective-permute-done.1.refs_8_ = bf16[96,768]{1,0:T(8,128)(2,1)S(1)} collective-permute-done((bf16[96,768]{1,0:T(8,128)(2,1)S(1)}, bf16[96,768]{1,0:T(8,128)(2,1)S(1)}, u32[]{:S(2)}, u32[]{:S(2)}) %collective-permute-start.1) | collective-permute-done | bytes 147488 | tf_op jit(solution)/shard_map/ppermute | solution.py:919
  25.7 1.5 collective-permute-start.2
  27.2 1.5 collective-permute-start.3
  29.2 4.1 %compress.2 = bf16[2,192,448]{2,1,0:T(8,128)(2,1)} custom-call(s32[2]{0:T(128)} %pad_add_fusion.place.refs_0_, s32[2,2]{1,0:T(2,128)} %rows_ref.5, s32[2]{0:T(128)} %groups.5, bf16[8,2,192,392]{3,2,1,0:T(8,128)(2,1)} %bitcast.54, bf16[8,2,192,392]{3,2,1,0:T(8,128)(2,1)} %bitcast.55, f32[2,192,8]{2,1,0:T(8,128)} %bitcast.47), custom_call_target="tpu_custom_call" | custom-call | flops 3000000000 | bytes 10000000 | tf_op jit(solution)/shard_map/compress/pallas_call | solution.py:616
  33.4 2.1 collective-permute-done.3
  37.3 1.9 collective-permute-start.14
  39.2 16.1 %attend.2 = (f32[2,196,768]{2,1,0:T(8,128)}, bf16[448,576]{1,0:T(8,128)(2,1)}, f32[2,2,448,448]{3,2,1,0:T(8,128)}, bf16[448,192]{1,0:T(8,128)(2,1)}) custom-call(s32[2]{0:T(128)} %pad_add_fusion.place.refs_0_, s32[2]{0:T(128)} %groups.5, bf16[196,768]{1,0:T(8,128)(2,1)} %get-tuple-element.66.refs_2_.refs_1_, bf16[196,768]{1,0:T(8,128)(2,1)} %copy-done.25, ...), custom_call_target="tpu_custom_call" | custom-call | flops 16000000000 | bytes 48000000 | tf_op jit(solution)/shard_map/attend/pallas_call | solution.py:53
  56.6 3.3 %collective-permute-start.8 = (bf16[196,768]{1,0:T(8,128)(2,1)S(1)}, bf16[196,768]{1,0:T(8,128)(2,1)S(1)}, u32[]{:S(2)}, u32[]{:S(2)}) collective-permute-start(bf16[196,768]{1,0:T(8,128)(2,1)S(1)} %copy-done.24), channel_id=1, source_target_pairs={{0,1},{1,0},{2,3},{3,2},{4,5},{5,4},{6,7},{7,6},{8,9},{9,8},{10,11... | collective-permute-start | bytes 903176 | tf_op jit(solution)/shard_map/ppermute | solution.py:922
  60.2 11.4 %collective-permute-done.8.refs_10_.refs_4_ = bf16[196,768]{1,0:T(8,128)(2,1)S(1)} collective-permute-done((bf16[196,768]{1,0:T(8,128)(2,1)S(1)}, bf16[196,768]{1,0:T(8,128)(2,1)S(1)}, u32[]{:S(2)}, u32[]{:S(2)}) %collective-permute-start.8) | collective-permute-done | bytes 301088 | tf_op jit(solution)/shard_map/ppermute | solution.py:922
  71.6 3.7 %collective-permute-done.7.refs_7_.refs_5_ = bf16[2,192,448]{2,1,0:T(8,128)(2,1)S(1)} collective-permute-done((bf16[2,192,448]{2,1,0:T(8,128)(2,1)S(1)}, bf16[2,192,448]{2,1,0:T(8,128)(2,1)S(1)}, u32[]{:S(2)}, u32[]{:S(2)}) %collective-permute-start.7) | collective-permute-done | bytes 344096 | tf_op jit(solution)/shard_map/ppermute | solution.py:919
  76.3 16.3 %attend.3 = (f32[196,768]{1,0:T(8,128)}, bf16[1,196,768]{2,1,0:T(8,128)(2,1)}, bf16[768,768]{1,0:T(8,128)(2,1)}, bf16[448,576]{1,0:T(8,128)(2,1)}, f32[2,2,448,448]{3,2,1,0:T(8,128)}, /*index=5*/bf16[448,192]{1,0:T(8,128)(2,1)}) custom-call(s32[2]{0:T(128)} %pad_add_fusion.place.refs_0_, s32[2]{0:T(128)} %groups.5, ...), custom_call_target="tpu_custom_call" | custom-call | flops 16000000000 | bytes 48000000 | tf_op jit(solution)/shard_map/attend/pallas_call | solution.py:53
  92.7 8.1 %collective-permute-done.9.refs_2_ = bf16[1,196,768]{2,1,0:T(8,128)(2,1)S(1)} collective-permute-done((bf16[1,196,768]{2,1,0:T(8,128)(2,1)}, bf16[1,196,768]{2,1,0:T(8,128)(2,1)S(1)}, u32[]{:S(2)}, u32[]{:S(2)}) %collective-permute-start.9) | collective-permute-done | bytes 301088 | tf_op jit(solution)/shard_map/ppermute | solution.py:922
  101.5 2.3 second_norm.1
  104.6 6.3 %collective-permute-done.10.refs_2_ = bf16[196,768]{1,0:T(8,128)(2,1)S(1)} collective-permute-done((bf16[196,768]{1,0:T(8,128)(2,1)}, bf16[196,768]{1,0:T(8,128)(2,1)S(1)}, u32[]{:S(2)}, u32[]{:S(2)}) %collective-permute-start.10) | collective-permute-done | bytes 301088 | tf_op jit(solution)/shard_map/ppermute | solution.py:922
  112.7 13.8 %mlp.1 = (f32[196,768]{1,0:T(8,128)}, bf16[1,196,768]{2,1,0:T(8,128)(2,1)}, f32[196,768]{1,0:T(8,128)}, bf16[1,196,768]{2,1,0:T(8,128)(2,1)}, bf16[2,392,768]{2,...) custom-call(s32[2]{0:T(128)} %pad_add_fusion.place.refs_0_, ...), custom_call_target="tpu_custom_call" | custom-call | flops 12000000000 | bytes 36000000 | tf_op jit(solution)/shard_map/mlp/pallas_call | solution.py:53
  126.4 4.5 %convolution_convert_fusion = bf16[2,768,768]{2,1,0:T(8,128)(2,1)} fusion(bf16[2,392,768]{2,1,0:T(8,128)(2,1)} %get-tuple-element.86, bf16[2,392,768]{2,1,0:T(8,128)(2,1)} %get-tuple-element.87), kind=kOutput, calls=%fused_computation | convolution fusion | flops 926023680 | bytes 4767744 | tf_op jit(solution)/shard_map/dot_general | solution.py:1106
  130.9 3.1 %convolution_convert_fusion.1 = bf16[2,768,768]{2,1,0:T(8,128)(2,1)S(1)} fusion(bf16[2,392,768]{2,1,0:T(8,128)(2,1)} %get-tuple-element.84, bf16[2,392,768]{2,1,0:T(8,128)(2,1)} %get-tuple-element.85), kind=kOutput, calls=%fused_computation.1 | convolution fusion | flops 926023680 | bytes 4767744 | tf_op jit(solution)/shard_map/dot_general | solution.py:1106
  134.0 1.6 collective-permute-done.18
  138.3 1.6 collective-permute-start.21
  140.5 1.7 collective-permute-start.16
  143.1 7.9 %collective-permute-done.16.refs_2_ = bf16[1,196,768]{2,1,0:T(8,128)(2,1)} collective-permute-done((bf16[1,196,768]{2,1,0:T(8,128)(2,1)}, bf16[1,196,768]{2,1,0:T(8,128)(2,1)}, u32[]{:S(2)}, u32[]{:S(2)}) %collective-permute-start.16) | collective-permute-done | bytes 301088 | tf_op jit(solution)/shard_map/ppermute | solution.py:922
  151.0 3.0 %second_back.1 = (f32[196,768]{1,0:T(8,128)}, bf16[196,768]{1,0:T(8,128)(2,1)}, f32[32,128]{1,0:T(8,128)}) custom-call(f32[196,768]{1,0:T(8,128)} %get-tuple-element.71.refs_0_.refs_5_, f32[196,768]{1,0:T(8,128)} %get-tuple-element.73.refs_1_, bf16[1,196,768]{2,1,0:T(8,128)(2,1)} %collective-permute-done.16.refs_2_, bf16[196,768]{1,0:T(8,128)(2,1)} %refs_3_.3, ...), custom_call_target="tpu_custom_call" | custom-call | flops 3000000000 | bytes 9000000 | tf_op jit(solution)/shard_map/second_back/pallas_call | solution.py:53
  154.1 1.7 collective-permute-start.17
  155.8 10.6 %collective-permute-done.21 = bf16[2,192,768]{2,1,0:T(8,128)(2,1)} collective-permute-done((bf16[2,192,768]{2,1,0:T(8,128)(2,1)}, bf16[2,192,768]{2,1,0:T(8,128)(2,1)}, u32[]{:S(2)}, u32[]{:S(2)}) %collective-permute-start.21) | collective-permute-done | bytes 589856 | tf_op jit(solution)/shard_map/ppermute | solution.py:925
  166.3 3.0 %convert_add_fusion = (f32[2,192,768]{2,1,0:T(8,128)S(1)}, f32[2,192,768]{2,1,0:T(8,128)}) fusion(bf16[2,192,768]{2,1,0:T(8,128)(2,1)} %collective-permute-done.22, bf16[2,192,768]{2,1,0:T(8,128)(2,1)} %collective-permute-done.21, bf16[2,192,768]{2,1,0:T(8,128)(2,1)} %collective-permute-done.20, bf16[2,768,768]{2,1,0:T(8,128)(2,1)S(1)} %collective-permute-done.18, ...), kind=kLoop, calls=%fused_computation.8 | loop fusion | flops 2654208 | bytes 5308420 | tf_op jit(solution)/shard_map/add | solution.py:992
  169.3 3.9 %collective-permute-start.23 = (bf16[192,768]{1,0:T(8,128)(2,1)S(1)}, bf16[192,768]{1,0:T(8,128)(2,1)S(1)}, u32[]{:S(2)}, u32[]{:S(2)}) collective-permute-start(bf16[192,768]{1,0:T(8,128)(2,1)S(1)} %fusion.2.refs_11_), channel_id=1, source_target_pairs={{0,2},{1,3},{2,0},{3,1},{4,6},{5,7},{6,4},{7,5},{8,10},{9,11},{10,... | collective-permute-start | bytes 884744 | tf_op jit(solution)/shard_map/ppermute | solution.py:919
  174.1 12.9 %scores_back.2 = (f32[448,576]{1,0:T(8,128)}, bf16[2,192,448]{2,1,0:T(8,128)(2,1)}, f32[96,128]{1,0:T(8,128)}, bf16[192,768]{1,0:T(8,128)(2,1)}) custom-call(s32[2]{0:T(128)} %pad_add_fusion.place.refs_0_, bf16[196,768]{1,0:T(8,128)(2,1)} %get-tuple-element.76.refs_1_, bf16[196,768]{1,0:T(8,128)(2,1)} %copy-done.27, ...), custom_call_target="tpu_custom_call" | custom-call | flops 12999999488 | bytes 39000000 | tf_op jit(solution)/shard_map/scores_back/pallas_call | solution.py:53
  187.0 12.7 %pool_back.2 = (f32[2,196,768]{2,1,0:T(8,128)}, bf16[384,768]{1,0:T(8,128)(2,1)}, bf16[384,768]{1,0:T(8,128)(2,1)}, f32[296,128]{1,0:T(8,128)}) custom-call(s32[2]{0:T(128)} %pad_add_fusion.place.refs_0_, bf16[196,768]{1,0:T(8,128)(2,1)} %get-tuple-element.66.refs_2_.refs_1_, bf16[196,768]{1,0:T(8,128)(2,1)} %copy-done.25, ...), custom_call_target="tpu_custom_call" | custom-call | flops 8999999488 | bytes 27000000 | tf_op jit(solution)/shard_map/pool_back/pallas_call | solution.py:53
  199.8 2.9 collective-permute-start.25
  202.7 13.0 %scores_back.3 = (f32[448,576]{1,0:T(8,128)}, bf16[2,192,448]{2,1,0:T(8,128)(2,1)}, f32[96,128]{1,0:T(8,128)}, bf16[192,768]{1,0:T(8,128)(2,1)}) custom-call(s32[2]{0:T(128)} %pad_add_fusion.place.refs_0_, bf16[196,768]{1,0:T(8,128)(2,1)} %get-tuple-element.76.refs_1_, bf16[196,768]{1,0:T(8,128)(2,1)} %copy-done.27, bf16[576,768]{1,0:T(8,128)(2,1)} %bitcast.49, ...), custom_call_target="tpu_custom_call" | custom-call | flops 12999999488 | bytes 39000000 | tf_op jit(solution)/shard_map/scores_back/pallas_call | solution.py:53
  220.1 2.5 collective-permute-done.39
  223.7 2.3 collective-permute-start.48
  229.4 12.8 %pool_back.3 = (f32[196,768]{1,0:T(8,128)}, bf16[1,196,768]{2,1,0:T(8,128)(2,1)}, bf16[384,768]{1,0:T(8,128)(2,1)}, bf16[384,768]{1,0:T(8,128)(2,1)}, f32[296,128]{1,0:T(8,128)}) custom-call(s32[2]{0:T(128)} %pad_add_fusion.place.refs_0_, bf16[196,768]{1,0:T(8,128)(2,1)} %get-tuple-element.66.refs_2_.refs_1_, bf16[196,768]{1,0:T(8,128)(2,1)} %copy-done.25, ...), custom_call_target="tpu_custom_call" | custom-call | flops 8999999488 | bytes 27000000 | tf_op jit(solution)/shard_map/pool_back/pallas_call | solution.py:53
  243.7 5.6 %compress_back.1.refs_11_ = f32[2,8,192]{2,1,0:T(8,128)} custom-call(s32[2]{0:T(128)} %pad_add_fusion.place.refs_0_, s32[2,2]{1,0:T(2,128)} %rows_ref.5, s32[2]{0:T(128)} %groups.5, bf16[8,2,192,392]{3,2,1,0:T(8,128)(2,1)} %bitcast.56, bf16[8,2,192,392]{3,2,1,0:T(8,128)(2,1)} %bitcast.57, bf16[8,2,192,392]{3,2,1,0:T(8,128)(2,1)} %bitcast.58, ...), custom_call_target="tpu_custom_call" | custom-call | flops 5000000000 | bytes 10000000 | tf_op jit(solution)/shard_map/compress_back/pallas_call | solution.py:651
  250.7 3.5 %first_back.1 = (f32[196,768]{1,0:T(8,128)}, bf16[196,768]{1,0:T(8,128)(2,1)}, f32[376,128]{1,0:T(8,128)}) custom-call(bf16[196,768]{1,0:T(8,128)(2,1)} %refs_0_.5, f32[196,768]{1,0:T(8,128)} %get-tuple-element.75.refs_1_, f32[6,128]{1,0:T(8,128)} %bitcast.70, f32[196,768]{1,0:T(8,128)} %get-tuple-element.101.refs_3_, bf16[1,196,768]{2,1,0:T(8,128)(2,1)} %copy-done.29, ...), custom_call_target="tpu_custom_call" | custom-call | flops 3000000000 | bytes 9000000 | tf_op jit(solution)/shard_map/first_back/pallas_call | solution.py:53
  260.5 3.0 %collective-permute-done.29 = f32[376,128]{1,0:T(8,128)S(1)} collective-permute-done((f32[376,128]{1,0:T(8,128)S(1)}, f32[376,128]{1,0:T(8,128)S(1)}, u32[]{:S(2)}, u32[]{:S(2)}) %collective-permute-start.29) | collective-permute-done | bytes 192544 | tf_op jit(solution)/shard_map/ppermute | solution.py:925
  265.9 3.0 %collective-permute-start.37 = (bf16[96,768]{1,0:T(8,128)(2,1)S(1)}, bf16[96,768]{1,0:T(8,128)(2,1)S(1)}, u32[]{:S(2)}, u32[]{:S(2)}) collective-permute-start(bf16[96,768]{1,0:T(8,128)(2,1)S(1)} %get-tuple-element.133), channel_id=1, source_target_pairs={{0,16},{4,20},{8,24},{12,28},{16,0},{20,4},{24,8},{28,12},{1,17},{... | collective-permute-start | bytes 442376 | tf_op jit(solution)/shard_map/ppermute | solution.py:925
  268.9 1.6 collective-permute-start.38
  271.3 1.7 close.1
  275.2 2.1 collective-permute-start.34
  278.1 1.5 collective-permute-start.44
  279.6 1.4 collective-permute-start.45
  283.2 2.5 collective-permute-done.45
  286.5 2.5 select_convert_fusion
  (172 shorter events, 46.5 us)
Async XLA Ops:
  1.8 33.8 %collective-permute-start.11 = (bf16[192,768]{1,0:T(8,128)(2,1)S(1)}, bf16[192,768]{1,0:T(8,128)(2,1)S(1)}, u32[]{:S(2)}, u32[]{:S(2)}) collective-permute-start(bf16[192,768]{1,0:T(8,128)(2,1)S(1)} %dynamic-slice_select_fusion.refs_9_), channel_id=1, source_target_pairs={{0,2},{1,3},{2,0},{3,1},{4,6},{5,7},{6,4},{7,5},{8,10},{9,11},{10,... | collective-permute-start | bytes 884744 | tf_op jit(solution)/shard_map/ppermute | solution.py:919
  7.0 18.7 %collective-permute-start.1 = (bf16[96,768]{1,0:T(8,128)(2,1)S(1)}, bf16[96,768]{1,0:T(8,128)(2,1)S(1)}, u32[]{:S(2)}, u32[]{:S(2)}) collective-permute-start(bf16[96,768]{1,0:T(8,128)(2,1)S(1)} %bitcast_select_fusion), channel_id=1, source_target_pairs={{0,2},{1,3},{2,0},{3,1},{4,6},{5,7},{6,4},{7,5},{8,10},{9,11},{10,... | collective-permute-start | bytes 442376 | tf_op jit(solution)/shard_map/ppermute | solution.py:919
  9.2 28.1 %collective-permute-start = (bf16[196,768]{1,0:T(8,128)(2,1)}, bf16[196,768]{1,0:T(8,128)(2,1)S(1)}, u32[]{:S(2)}, u32[]{:S(2)}) collective-permute-start(bf16[196,768]{1,0:T(8,128)(2,1)} %get-tuple-element.66.refs_2_.refs_1_), channel_id=1, source_target_pairs={{0,1},{1,0},{2,3},{3,2},{4,5},{5,4},{6,7},{7,6},{8,9},{9,8},{10,11... | collective-permute-start | bytes 903176 | tf_op jit(solution)/shard_map/ppermute | solution.py:922
  25.7 7.6 %collective-permute-start.2 = (bf16[96,768]{1,0:T(8,128)(2,1)S(1)}, bf16[96,768]{1,0:T(8,128)(2,1)S(1)}, u32[]{:S(2)}, u32[]{:S(2)}) collective-permute-start(bf16[96,768]{1,0:T(8,128)(2,1)S(1)} %collective-permute-done.1.refs_8_), channel_id=1, source_target_pairs={{0,8},{4,12},{8,0},{12,4},{16,24},{20,28},{24,16},{28,20},{1,9},{5... | collective-permute-start | bytes 442376 | tf_op jit(solution)/shard_map/ppermute | solution.py:925
  27.2 8.2 %collective-permute-start.3 = (bf16[96,768]{1,0:T(8,128)(2,1)S(1)}, bf16[96,768]{1,0:T(8,128)(2,1)S(1)}, u32[]{:S(2)}, u32[]{:S(2)}) collective-permute-start(bf16[96,768]{1,0:T(8,128)(2,1)S(1)} %collective-permute-done.1.refs_8_), channel_id=1, source_target_pairs={{0,16},{4,20},{8,24},{12,28},{16,0},{20,4},{24,8},{28,12},{1,17},{... | collective-permute-start | bytes 442376 | tf_op jit(solution)/shard_map/ppermute | solution.py:925
  28.8 6.6 %collective-permute-start.4 = (bf16[96,768]{1,0:T(8,128)(2,1)S(1)}, bf16[96,768]{1,0:T(8,128)(2,1)S(1)}, u32[]{:S(2)}, u32[]{:S(2)}) collective-permute-start(bf16[96,768]{1,0:T(8,128)(2,1)S(1)} %collective-permute-done.1.refs_8_), channel_id=1, source_target_pairs={{0,24},{4,28},{8,16},{12,20},{16,8},{20,12},{24,0},{28,4},{1,25},{... | collective-permute-start | bytes 442376 | tf_op jit(solution)/shard_map/ppermute | solution.py:925
  33.3 26.9 %collective-permute-start.6 = (f32[296,128]{1,0:T(8,128)S(1)}, f32[296,128]{1,0:T(8,128)S(1)}, u32[]{:S(2)}, u32[]{:S(2)}) collective-permute-start(f32[296,128]{1,0:T(8,128)S(1)} %copy-done.32), channel_id=1, source_target_pairs={{0,2},{1,3},{2,0},{3,1},{4,6},{5,7},{6,4},{7,5},{8,10},{9,11},{10,... | collective-permute-start | bytes 454664 | tf_op jit(solution)/shard_map/ppermute | solution.py:919
  35.6 39.8 %collective-permute-start.5 = (bf16[384,768]{1,0:T(8,128)(2,1)S(1)}, bf16[384,768]{1,0:T(8,128)(2,1)S(1)}, u32[]{:S(2)}, u32[]{:S(2)}) collective-permute-start(bf16[384,768]{1,0:T(8,128)(2,1)S(1)} %pad_maximum_fusion.2.refs_4_), channel_id=1, source_target_pairs={{0,4},{4,0},{8,12},{12,8},{16,20},{20,16},{24,28},{28,24},{1,5},{5... | collective-permute-start | bytes 1769480 | tf_op jit(solution)/shard_map/ppermute | solution.py:925
  35.6 19.7 %collective-permute-start.12 = (bf16[192,768]{1,0:T(8,128)(2,1)S(1)}, bf16[192,768]{1,0:T(8,128)(2,1)S(1)}, u32[]{:S(2)}, u32[]{:S(2)}) collective-permute-start(bf16[192,768]{1,0:T(8,128)(2,1)S(1)} %collective-permute-done.11), channel_id=1, source_target_pairs={{0,8},{4,12},{8,0},{12,4},{16,24},{20,28},{24,16},{28,20},{1,9},{5... | collective-permute-start | bytes 884744 | tf_op jit(solution)/shard_map/ppermute | solution.py:925
  36.3 20.2 %collective-permute-start.13 = (bf16[192,768]{1,0:T(8,128)(2,1)S(1)}, bf16[192,768]{1,0:T(8,128)(2,1)S(1)}, u32[]{:S(2)}, u32[]{:S(2)}) collective-permute-start(bf16[192,768]{1,0:T(8,128)(2,1)S(1)} %collective-permute-done.11), channel_id=1, source_target_pairs={{0,16},{4,20},{8,24},{12,28},{16,0},{20,4},{24,8},{28,12},{1,17},{... | collective-permute-start | bytes 884744 | tf_op jit(solution)/shard_map/ppermute | solution.py:925
  37.3 22.6 %collective-permute-start.14 = (bf16[192,768]{1,0:T(8,128)(2,1)S(1)}, bf16[192,768]{1,0:T(8,128)(2,1)S(1)}, u32[]{:S(2)}, u32[]{:S(2)}) collective-permute-start(bf16[192,768]{1,0:T(8,128)(2,1)S(1)} %collective-permute-done.11), channel_id=1, source_target_pairs={{0,24},{4,28},{8,16},{12,20},{16,8},{20,12},{24,0},{28,4},{1,25},{... | collective-permute-start | bytes 884744 | tf_op jit(solution)/shard_map/ppermute | solution.py:925
  55.4 20.0 %collective-permute-start.7 = (bf16[2,192,448]{2,1,0:T(8,128)(2,1)S(1)}, bf16[2,192,448]{2,1,0:T(8,128)(2,1)S(1)}, u32[]{:S(2)}, u32[]{:S(2)}) collective-permute-start(bf16[2,192,448]{2,1,0:T(8,128)(2,1)S(1)} %copy-done.23), channel_id=1, source_target_pairs={{0,2},{1,3},{2,0},{3,1},{4,6},{5,7},{6,4},{7,5},{8,10},{9,11},{10,... | collective-permute-start | bytes 1032200 | tf_op jit(solution)/shard_map/ppermute | solution.py:919
  56.6 15.1 %collective-permute-start.8 = (bf16[196,768]{1,0:T(8,128)(2,1)S(1)}, bf16[196,768]{1,0:T(8,128)(2,1)S(1)}, u32[]{:S(2)}, u32[]{:S(2)}) collective-permute-start(bf16[196,768]{1,0:T(8,128)(2,1)S(1)} %copy-done.24), channel_id=1, source_target_pairs={{0,1},{1,0},{2,3},{3,2},{4,5},{5,4},{6,7},{7,6},{8,9},{9,8},{10,11... | collective-permute-start | bytes 903176 | tf_op jit(solution)/shard_map/ppermute | solution.py:922
  60.1 50.8 %collective-permute-start.15 = (bf16[768,768]{1,0:T(8,128)(2,1)S(1)}, bf16[768,768]{1,0:T(8,128)(2,1)S(1)}, u32[]{:S(2)}, u32[]{:S(2)}) collective-permute-start(bf16[768,768]{1,0:T(8,128)(2,1)S(1)} %pad_maximum_fusion.refs_7_), channel_id=1, source_target_pairs={{0,4},{4,0},{8,12},{12,8},{16,20},{20,16},{24,28},{28,24},{1,5},{5... | collective-permute-start | bytes 3538952 | tf_op jit(solution)/shard_map/ppermute | solution.py:925
  92.6 8.2 %collective-permute-start.9 = (bf16[1,196,768]{2,1,0:T(8,128)(2,1)}, bf16[1,196,768]{2,1,0:T(8,128)(2,1)S(1)}, u32[]{:S(2)}, u32[]{:S(2)}) collective-permute-start(bf16[1,196,768]{2,1,0:T(8,128)(2,1)} %get-tuple-element.70), channel_id=1, source_target_pairs={{0,1},{1,0},{2,3},{3,2},{4,5},{5,4},{6,7},{7,6},{8,9},{9,8},{10,11... | collective-permute-start | bytes 903176 | tf_op jit(solution)/shard_map/ppermute | solution.py:922
  103.8 7.2 %collective-permute-start.10 = (bf16[196,768]{1,0:T(8,128)(2,1)}, bf16[196,768]{1,0:T(8,128)(2,1)S(1)}, u32[]{:S(2)}, u32[]{:S(2)}) collective-permute-start(bf16[196,768]{1,0:T(8,128)(2,1)} %get-tuple-element.72.refs_1_), channel_id=1, source_target_pairs={{0,1},{1,0},{2,3},{3,2},{4,5},{5,4},{6,7},{7,6},{8,9},{9,8},{10,11... | collective-permute-start | bytes 903176 | tf_op jit(solution)/shard_map/ppermute | solution.py:922
  137.0 18.8 %collective-permute-start.20 = (bf16[2,192,768]{2,1,0:T(8,128)(2,1)S(1)}, bf16[2,192,768]{2,1,0:T(8,128)(2,1)}, u32[]{:S(2)}, u32[]{:S(2)}) collective-permute-start(bf16[2,192,768]{2,1,0:T(8,128)(2,1)S(1)} %get-tuple-element.120.refs_10_), channel_id=1, source_target_pairs={{0,8},{4,12},{8,0},{12,4},{16,24},{20,28},{24,16},{28,20},{1,9},{5... | collective-permute-start | bytes 1769480 | tf_op jit(solution)/shard_map/ppermute | solution.py:925
  138.3 28.0 %collective-permute-start.21 = (bf16[2,192,768]{2,1,0:T(8,128)(2,1)}, bf16[2,192,768]{2,1,0:T(8,128)(2,1)}, u32[]{:S(2)}, u32[]{:S(2)}) collective-permute-start(bf16[2,192,768]{2,1,0:T(8,128)(2,1)} %get-tuple-element.122.refs_11_), channel_id=1, source_target_pairs={{0,16},{4,20},{8,24},{12,28},{16,0},{20,4},{24,8},{28,12},{1,17},{... | collective-permute-start | bytes 1769480 | tf_op jit(solution)/shard_map/ppermute | solution.py:925
  139.9 26.4 %collective-permute-start.22 = (bf16[2,192,768]{2,1,0:T(8,128)(2,1)S(1)}, bf16[2,192,768]{2,1,0:T(8,128)(2,1)}, u32[]{:S(2)}, u32[]{:S(2)}) collective-permute-start(bf16[2,192,768]{2,1,0:T(8,128)(2,1)S(1)} %get-tuple-element.121.refs_12_), channel_id=1, source_target_pairs={{0,24},{4,28},{8,16},{12,20},{16,8},{20,12},{24,0},{28,4},{1,25},{... | collective-permute-start | bytes 1769480 | tf_op jit(solution)/shard_map/ppermute | solution.py:925
  140.5 10.5 %collective-permute-start.16 = (bf16[1,196,768]{2,1,0:T(8,128)(2,1)}, bf16[1,196,768]{2,1,0:T(8,128)(2,1)}, u32[]{:S(2)}, u32[]{:S(2)}) collective-permute-start(bf16[1,196,768]{2,1,0:T(8,128)(2,1)} %get-tuple-element.74), channel_id=1, source_target_pairs={{0,1},{1,0},{2,3},{3,2},{4,5},{5,4},{6,7},{7,6},{8,9},{9,8},{10,11... | collective-permute-start | bytes 903176 | tf_op jit(solution)/shard_map/ppermute | solution.py:922
  142.1 31.1 %collective-permute-start.19 = (bf16[1,196,768]{2,1,0:T(8,128)(2,1)}, bf16[1,196,768]{2,1,0:T(8,128)(2,1)S(1)}, u32[]{:S(2)}, u32[]{:S(2)}) collective-permute-start(bf16[1,196,768]{2,1,0:T(8,128)(2,1)} %get-tuple-element.88), channel_id=1, source_target_pairs={{0,1},{1,0},{2,3},{3,2},{4,5},{5,4},{6,7},{7,6},{8,9},{9,8},{10,11... | collective-permute-start | bytes 903176 | tf_op jit(solution)/shard_map/ppermute | solution.py:922
  154.1 19.2 %collective-permute-start.17 = (bf16[196,768]{1,0:T(8,128)(2,1)}, bf16[196,768]{1,0:T(8,128)(2,1)S(1)}, u32[]{:S(2)}, u32[]{:S(2)}) collective-permute-start(bf16[196,768]{1,0:T(8,128)(2,1)} %get-tuple-element.76.refs_1_), channel_id=1, source_target_pairs={{0,1},{1,0},{2,3},{3,2},{4,5},{5,4},{6,7},{7,6},{8,9},{9,8},{10,11... | collective-permute-start | bytes 903176 | tf_op jit(solution)/shard_map/ppermute | solution.py:922
  169.3 48.6 %collective-permute-start.23 = (bf16[192,768]{1,0:T(8,128)(2,1)S(1)}, bf16[192,768]{1,0:T(8,128)(2,1)S(1)}, u32[]{:S(2)}, u32[]{:S(2)}) collective-permute-start(bf16[192,768]{1,0:T(8,128)(2,1)S(1)} %fusion.2.refs_11_), channel_id=1, source_target_pairs={{0,2},{1,3},{2,0},{3,1},{4,6},{5,7},{6,4},{7,5},{8,10},{9,11},{10,... | collective-permute-start | bytes 884744 | tf_op jit(solution)/shard_map/ppermute | solution.py:919
  199.7 15.9 %collective-permute-start.24 = (bf16[384,768]{1,0:T(8,128)(2,1)}, bf16[384,768]{1,0:T(8,128)(2,1)S(1)}, u32[]{:S(2)}, u32[]{:S(2)}) collective-permute-start(bf16[384,768]{1,0:T(8,128)(2,1)} %get-tuple-element.98), channel_id=1, source_target_pairs={{0,4},{4,0},{8,12},{12,8},{16,20},{20,16},{24,28},{28,24},{1,5},{5... | collective-permute-start | bytes 1769480 | tf_op jit(solution)/shard_map/ppermute | solution.py:925
  199.7 28.9 %collective-permute-start.26 = (f32[296,128]{1,0:T(8,128)}, f32[296,128]{1,0:T(8,128)S(1)}, u32[]{:S(2)}, u32[]{:S(2)}) collective-permute-start(f32[296,128]{1,0:T(8,128)} %get-tuple-element.100), channel_id=1, source_target_pairs={{0,2},{1,3},{2,0},{3,1},{4,6},{5,7},{6,4},{7,5},{8,10},{9,11},{10,... | collective-permute-start | bytes 454664 | tf_op jit(solution)/shard_map/ppermute | solution.py:919
  199.8 28.8 %collective-permute-start.25 = (bf16[2,192,448]{2,1,0:T(8,128)(2,1)S(1)}, bf16[2,192,448]{2,1,0:T(8,128)(2,1)S(1)}, u32[]{:S(2)}, u32[]{:S(2)}) collective-permute-start(bf16[2,192,448]{2,1,0:T(8,128)(2,1)S(1)} %copy-done.21), channel_id=1, source_target_pairs={{0,2},{1,3},{2,0},{3,1},{4,6},{5,7},{6,4},{7,5},{8,10},{9,11},{10,... | collective-permute-start | bytes 1032200 | tf_op jit(solution)/shard_map/ppermute | solution.py:919
  215.8 6.8 %collective-permute-start.39 = (bf16[96,768]{1,0:T(8,128)(2,1)S(1)}, bf16[96,768]{1,0:T(8,128)(2,1)S(1)}, u32[]{:S(2)}, u32[]{:S(2)}) collective-permute-start(bf16[96,768]{1,0:T(8,128)(2,1)S(1)} %get-tuple-element.134.refs_13_), channel_id=1, source_target_pairs={{0,8},{4,12},{8,0},{12,4},{16,24},{20,28},{24,16},{28,20},{1,9},{5... | collective-permute-start | bytes 442376 | tf_op jit(solution)/shard_map/ppermute | solution.py:925
  216.9 6.7 %collective-permute-start.40 = (bf16[96,768]{1,0:T(8,128)(2,1)S(1)}, bf16[96,768]{1,0:T(8,128)(2,1)S(1)}, u32[]{:S(2)}, u32[]{:S(2)}) collective-permute-start(bf16[96,768]{1,0:T(8,128)(2,1)S(1)} %get-tuple-element.136.refs_14_), channel_id=1, source_target_pairs={{0,16},{4,20},{8,24},{12,28},{16,0},{20,4},{24,8},{28,12},{1,17},{... | collective-permute-start | bytes 442376 | tf_op jit(solution)/shard_map/ppermute | solution.py:925
  218.0 8.8 %collective-permute-start.41 = (bf16[96,768]{1,0:T(8,128)(2,1)S(1)}, bf16[96,768]{1,0:T(8,128)(2,1)S(1)}, u32[]{:S(2)}, u32[]{:S(2)}) collective-permute-start(bf16[96,768]{1,0:T(8,128)(2,1)S(1)} %get-tuple-element.135.refs_15_), channel_id=1, source_target_pairs={{0,24},{4,28},{8,16},{12,20},{16,8},{20,12},{24,0},{28,4},{1,25},{... | collective-permute-start | bytes 442376 | tf_op jit(solution)/shard_map/ppermute | solution.py:925
  222.6 31.5 %collective-permute-start.47 = (bf16[192,768]{1,0:T(8,128)(2,1)}, bf16[192,768]{1,0:T(8,128)(2,1)S(1)}, u32[]{:S(2)}, u32[]{:S(2)}) collective-permute-start(bf16[192,768]{1,0:T(8,128)(2,1)} %fusion.1.refs_11_), channel_id=1, source_target_pairs={{0,8},{4,12},{8,0},{12,4},{16,24},{20,28},{24,16},{28,20},{1,9},{5... | collective-permute-start | bytes 884744 | tf_op jit(solution)/shard_map/ppermute | solution.py:925
  223.7 30.5 %collective-permute-start.48 = (bf16[192,768]{1,0:T(8,128)(2,1)}, bf16[192,768]{1,0:T(8,128)(2,1)S(1)}, u32[]{:S(2)}, u32[]{:S(2)}) collective-permute-start(bf16[192,768]{1,0:T(8,128)(2,1)} %fusion.1.refs_11_), channel_id=1, source_target_pairs={{0,16},{4,20},{8,24},{12,28},{16,0},{20,4},{24,8},{28,12},{1,17},{... | collective-permute-start | bytes 884744 | tf_op jit(solution)/shard_map/ppermute | solution.py:925
  226.7 27.4 %collective-permute-start.49 = (bf16[192,768]{1,0:T(8,128)(2,1)}, bf16[192,768]{1,0:T(8,128)(2,1)S(1)}, u32[]{:S(2)}, u32[]{:S(2)}) collective-permute-start(bf16[192,768]{1,0:T(8,128)(2,1)} %fusion.1.refs_11_), channel_id=1, source_target_pairs={{0,24},{4,28},{8,16},{12,20},{16,8},{20,12},{24,0},{28,4},{1,25},{... | collective-permute-start | bytes 884744 | tf_op jit(solution)/shard_map/ppermute | solution.py:925
  242.3 7.7 %collective-permute-start.27 = (bf16[1,196,768]{2,1,0:T(8,128)(2,1)}, bf16[1,196,768]{2,1,0:T(8,128)(2,1)S(1)}, u32[]{:S(2)}, u32[]{:S(2)}) collective-permute-start(bf16[1,196,768]{2,1,0:T(8,128)(2,1)} %get-tuple-element.102), channel_id=1, source_target_pairs={{0,1},{1,0},{2,3},{3,2},{4,5},{5,4},{6,7},{7,6},{8,9},{9,8},{10,11... | collective-permute-start | bytes 903176 | tf_op jit(solution)/shard_map/ppermute | solution.py:922
  249.3 10.2 %collective-permute-start.35 = (bf16[384,768]{1,0:T(8,128)(2,1)S(1)}, bf16[384,768]{1,0:T(8,128)(2,1)S(1)}, u32[]{:S(2)}, u32[]{:S(2)}) collective-permute-start(bf16[384,768]{1,0:T(8,128)(2,1)S(1)} %copy-done.18), channel_id=1, source_target_pairs={{0,4},{4,0},{8,12},{12,8},{16,20},{20,16},{24,28},{28,24},{1,5},{5... | collective-permute-start | bytes 1769480 | tf_op jit(solution)/shard_map/ppermute | solution.py:925
  255.8 7.7 %collective-permute-start.29 = (f32[376,128]{1,0:T(8,128)S(1)}, f32[376,128]{1,0:T(8,128)S(1)}, u32[]{:S(2)}, u32[]{:S(2)}) collective-permute-start(f32[376,128]{1,0:T(8,128)S(1)} %add.203), channel_id=1, source_target_pairs={{0,8},{4,12},{8,0},{12,4},{16,24},{20,28},{24,16},{28,20},{1,9},{5... | collective-permute-start | bytes 577544 | tf_op jit(solution)/shard_map/ppermute | solution.py:925
  256.9 9.0 %collective-permute-start.30 = (f32[376,128]{1,0:T(8,128)S(1)}, f32[376,128]{1,0:T(8,128)S(1)}, u32[]{:S(2)}, u32[]{:S(2)}) collective-permute-start(f32[376,128]{1,0:T(8,128)S(1)} %add.203), channel_id=1, source_target_pairs={{0,16},{4,20},{8,24},{12,28},{16,0},{20,4},{24,8},{28,12},{1,17},{... | collective-permute-start | bytes 577544 | tf_op jit(solution)/shard_map/ppermute | solution.py:925
  257.9 11.0 %collective-permute-start.31 = (f32[376,128]{1,0:T(8,128)S(1)}, f32[376,128]{1,0:T(8,128)S(1)}, u32[]{:S(2)}, u32[]{:S(2)}) collective-permute-start(f32[376,128]{1,0:T(8,128)S(1)} %add.203), channel_id=1, source_target_pairs={{0,24},{4,28},{8,16},{12,20},{16,8},{20,12},{24,0},{28,4},{1,25},{... | collective-permute-start | bytes 577544 | tf_op jit(solution)/shard_map/ppermute | solution.py:925
  259.5 27.1 %collective-permute-start.50 = (bf16[768,768]{1,0:T(8,128)(2,1)S(1)}, bf16[768,768]{1,0:T(8,128)(2,1)S(1)}, u32[]{:S(2)}, u32[]{:S(2)}) collective-permute-start(bf16[768,768]{1,0:T(8,128)(2,1)S(1)} %pad_maximum_fusion.1), channel_id=1, source_target_pairs={{0,4},{4,0},{8,12},{12,8},{16,20},{20,16},{24,28},{28,24},{1,5},{5... | collective-permute-start | bytes 3538952 | tf_op jit(solution)/shard_map/ppermute | solution.py:925
  259.5 13.4 %collective-permute-start.42 = (bf16[96,768]{1,0:T(8,128)(2,1)S(1)}, bf16[96,768]{1,0:T(8,128)(2,1)S(1)}, u32[]{:S(2)}, u32[]{:S(2)}) collective-permute-start(bf16[96,768]{1,0:T(8,128)(2,1)S(1)} %get-tuple-element.116), channel_id=1, source_target_pairs={{0,2},{1,3},{2,0},{3,1},{4,6},{5,7},{6,4},{7,5},{8,10},{9,11},{10,... | collective-permute-start | bytes 442376 | tf_op jit(solution)/shard_map/ppermute | solution.py:919
  263.5 9.7 %collective-permute-start.36 = (bf16[96,768]{1,0:T(8,128)(2,1)S(1)}, bf16[96,768]{1,0:T(8,128)(2,1)S(1)}, u32[]{:S(2)}, u32[]{:S(2)}) collective-permute-start(bf16[96,768]{1,0:T(8,128)(2,1)S(1)} %get-tuple-element.131), channel_id=1, source_target_pairs={{0,8},{4,12},{8,0},{12,4},{16,24},{20,28},{24,16},{28,20},{1,9},{5... | collective-permute-start | bytes 442376 | tf_op jit(solution)/shard_map/ppermute | solution.py:925
  265.9 9.3 %collective-permute-start.37 = (bf16[96,768]{1,0:T(8,128)(2,1)S(1)}, bf16[96,768]{1,0:T(8,128)(2,1)S(1)}, u32[]{:S(2)}, u32[]{:S(2)}) collective-permute-start(bf16[96,768]{1,0:T(8,128)(2,1)S(1)} %get-tuple-element.133), channel_id=1, source_target_pairs={{0,16},{4,20},{8,24},{12,28},{16,0},{20,4},{24,8},{28,12},{1,17},{... | collective-permute-start | bytes 442376 | tf_op jit(solution)/shard_map/ppermute | solution.py:925
  268.9 8.4 %collective-permute-start.38 = (bf16[96,768]{1,0:T(8,128)(2,1)S(1)}, bf16[96,768]{1,0:T(8,128)(2,1)S(1)}, u32[]{:S(2)}, u32[]{:S(2)}) collective-permute-start(bf16[96,768]{1,0:T(8,128)(2,1)S(1)} %get-tuple-element.132), channel_id=1, source_target_pairs={{0,24},{4,28},{8,16},{12,20},{16,8},{20,12},{24,0},{28,4},{1,25},{... | collective-permute-start | bytes 442376 | tf_op jit(solution)/shard_map/ppermute | solution.py:925
  272.9 5.2 %collective-permute-start.32 = (f32[48,128]{1,0:T(8,128)S(1)}, f32[48,128]{1,0:T(8,128)S(1)}, u32[]{:S(2)}, u32[]{:S(2)}) collective-permute-start(f32[48,128]{1,0:T(8,128)S(1)} %slice.55), channel_id=1, source_target_pairs={{0,1},{1,0},{2,3},{3,2},{4,5},{5,4},{6,7},{7,6},{8,9},{9,8},{10,11... | collective-permute-start | bytes 73736 | tf_op jit(solution)/shard_map/ppermute | solution.py:922
  273.2 6.4 %collective-permute-start.33 = (f32[48,128]{1,0:T(8,128)S(1)}, f32[48,128]{1,0:T(8,128)S(1)}, u32[]{:S(2)}, u32[]{:S(2)}) collective-permute-start(f32[48,128]{1,0:T(8,128)S(1)} %slice.55), channel_id=1, source_target_pairs={{0,2},{1,3},{2,0},{3,1},{4,6},{5,7},{6,4},{7,5},{8,10},{9,11},{10,... | collective-permute-start | bytes 73736 | tf_op jit(solution)/shard_map/ppermute | solution.py:922
  275.2 5.9 %collective-permute-start.34 = (f32[48,128]{1,0:T(8,128)S(1)}, f32[48,128]{1,0:T(8,128)S(1)}, u32[]{:S(2)}, u32[]{:S(2)}) collective-permute-start(f32[48,128]{1,0:T(8,128)S(1)} %slice.55), channel_id=1, source_target_pairs={{0,3},{1,2},{2,1},{3,0},{4,7},{5,6},{6,5},{7,4},{8,11},{9,10},{10,... | collective-permute-start | bytes 73736 | tf_op jit(solution)/shard_map/ppermute | solution.py:922
  277.4 5.2 %collective-permute-start.43 = (bf16[96,768]{1,0:T(8,128)(2,1)S(1)}, bf16[96,768]{1,0:T(8,128)(2,1)S(1)}, u32[]{:S(2)}, u32[]{:S(2)}) collective-permute-start(bf16[96,768]{1,0:T(8,128)(2,1)S(1)} %add_convert_fusion.3), channel_id=1, source_target_pairs={{0,8},{4,12},{8,0},{12,4},{16,24},{20,28},{24,16},{28,20},{1,9},{5... | collective-permute-start | bytes 442376 | tf_op jit(solution)/shard_map/ppermute | solution.py:925
  278.1 5.1 %collective-permute-start.44 = (bf16[96,768]{1,0:T(8,128)(2,1)S(1)}, bf16[96,768]{1,0:T(8,128)(2,1)S(1)}, u32[]{:S(2)}, u32[]{:S(2)}) collective-permute-start(bf16[96,768]{1,0:T(8,128)(2,1)S(1)} %add_convert_fusion.3), channel_id=1, source_target_pairs={{0,16},{4,20},{8,24},{12,28},{16,0},{20,4},{24,8},{28,12},{1,17},{... | collective-permute-start | bytes 442376 | tf_op jit(solution)/shard_map/ppermute | solution.py:925
  279.6 6.1 %collective-permute-start.45 = (bf16[96,768]{1,0:T(8,128)(2,1)S(1)}, bf16[96,768]{1,0:T(8,128)(2,1)S(1)}, u32[]{:S(2)}, u32[]{:S(2)}) collective-permute-start(bf16[96,768]{1,0:T(8,128)(2,1)S(1)} %add_convert_fusion.3), channel_id=1, source_target_pairs={{0,24},{4,28},{8,16},{12,20},{16,8},{20,12},{24,0},{28,4},{1,25},{... | collective-permute-start | bytes 442376 | tf_op jit(solution)/shard_map/ppermute | solution.py:925
  (38 other events, 298.4 us)
